TPU v7x, 256 devices: a whole 4x4x8 slice. The times are simulated.
256 devices in a mesh: row: 16 (over y_lo, x, core), col: 16 (over y_hi, z).
Axes of the slice: x: 4, y: 4 (y_hi: 2, y_lo: 2; y = y_hi * 2 + y_lo), z: 8, core: 2. Of those that a mesh axis runs over, the one named last changes fastest.
Arguments:
- query: bfloat16 [2, 96, 1024, 128], P(None, 'row', 'col'), may hold values from -6 to 6
- key: bfloat16 [2, 96, 1024, 128], P(None, 'row', 'col'), may hold values from -6 to 6
- value: bfloat16 [2, 96, 1024, 128], P(None, 'row', 'col'), may hold values from -6 to 6
- grad_out: bfloat16 [2, 96, 1024, 128], P(None, 'row', 'col'), may hold values from -1.5 to 1.5
- pair_bias: bfloat16 [2, 4, 1024, 1024], P(None, None, 'col'), may hold values from -6 to 250
- crop_lengths: int32 [2], replicated, may hold values from 256 to 1024, as said below
Outputs:
- grad_query: float32 [2, 96, 1024, 128], P(None, 'row', 'col')
- grad_key: float32 [2, 96, 1024, 128], P(None, 'row', 'col')
- grad_value: float32 [2, 96, 1024, 128], P(None, 'row', 'col')
- grad_bias: float32 [2, 4, 1024, 1024], P(None, None, 'col', 'row')
Inputs may be any that keep to these rules, and one draw needn't show every extreme that they name: `crop_lengths`: every crop has at least 256 valid residues, and some crop has all 1024.
All inputs are finite; a program needn't handle non-finite values.
Results may differ from a plain program's by a relative error of at most 0.0031.
Values may be sent and summed in bfloat16 or wider, within the bound.
A program may use at most 128 MiB of HBM per device.

v0:
```python
import jax
import jax.numpy as jnp
from jax import lax
from jax.sharding import PartitionSpec as P

H = 4
HD = 32


def from_behind(block, axis, distance):
    devices = range(lax.axis_size(axis))
    route = [((i - distance) % len(devices), i) for i in devices]
    return lax.ppermute(block, axis, route)


def split_heads(tensor):
    return tensor.reshape(tensor.shape[:-1] + (H, HD))


def pair_products(left, right):
    return jnp.einsum(
        "crjhd,crkhd->crhjk",
        split_heads(left),
        split_heads(right),
        preferred_element_type=jnp.float32,
    )


def tile_scores(query_blk, key_blk, bias_blk, key_start, crop_lengths):
    scores = (
        pair_products(query_blk, key_blk) * HD ** (-0.5) + bias_blk.astype(jnp.float32)[:, None]
    )
    tile_width = key_blk.shape[2]
    columns = key_start + lax.iota(jnp.int32, tile_width)
    key_valid = (columns[None, :] < crop_lengths[:, None])[:, None, None, None, :]
    return (jnp.where(key_valid, scores, -1e30), key_valid)


def tile_probs(
    query_blk, key_blk, value_blk, grad_blk, bias_blk, log_total, delta, key_start, crop_lengths
):
    scores, key_valid = tile_scores(query_blk, key_blk, bias_blk, key_start, crop_lengths)
    probs = jnp.where(key_valid, jnp.exp(scores - log_total[..., None]), 0.0)
    dprobs = pair_products(grad_blk, value_blk)
    dscores = probs * (dprobs - delta[..., None])
    return (probs, dscores)


def rotate_tiles(key_tile, value_tile):
    return from_behind((key_tile, value_tile), "col", 1)


def send_grads(key_sum, value_sum):
    return from_behind((key_sum, value_sum), "col", 1)


def per_device(query, key, value, grad_out, pair_bias, crop_lengths):
    count = lax.axis_size("col")
    my_index = lax.axis_index("col")
    tile_width = key.shape[2]
    stat_shape = (query.shape[0], query.shape[1], H, query.shape[2])
    head_shape = key.shape[:-1] + (H, HD)
    scale = HD ** (-0.5)

    def stat_update(turn_index, key_tile, value_tile, row_max, row_total, weighted):
        owner_index = jnp.mod(my_index - turn_index, count)
        key_start = owner_index * tile_width
        bias_blk = lax.dynamic_slice_in_dim(pair_bias, key_start, tile_width, 3)
        scores, key_valid = tile_scores(query, key_tile, bias_blk, key_start, crop_lengths)
        dprobs = pair_products(grad_out, value_tile)
        new_max = jnp.maximum(row_max, jnp.max(scores, axis=-1))
        rescale = jnp.exp(row_max - new_max)
        expped = jnp.exp(scores - new_max[..., None])
        row_total = row_total * rescale + jnp.sum(expped, axis=-1)
        weighted = weighted * rescale + jnp.sum(expped * dprobs, axis=-1)
        return (new_max, row_total, weighted)

    def stat_turn(turn_index, state_tuple):
        key_tile, value_tile, row_max, row_total, weighted, stored = state_tuple
        row_max, row_total, weighted = stat_update(
            turn_index, key_tile, value_tile, row_max, row_total, weighted
        )
        key_tile, value_tile = rotate_tiles(key_tile, value_tile)
        return (key_tile, value_tile, row_max, row_total, weighted, stored)

    start_state = (
        key,
        value,
        jnp.full(stat_shape, -1e30, jnp.float32),
        jnp.zeros(stat_shape, jnp.float32),
        jnp.zeros(stat_shape, jnp.float32),
        None,
    )
    key_tile, value_tile, row_max, row_total, weighted, stored = lax.fori_loop(
        0, count - 1, stat_turn, start_state
    )
    row_max, row_total, weighted = stat_update(
        count - 1, key_tile, value_tile, row_max, row_total, weighted
    )
    log_total = row_max + jnp.log(row_total)
    delta = weighted / row_total

    def query_update(turn_index, key_tile, value_tile, query_sum, bias_part):
        owner_index = jnp.mod(my_index - turn_index, count)
        key_start = owner_index * tile_width
        bias_blk = lax.dynamic_slice_in_dim(pair_bias, key_start, tile_width, 3)
        probs, dscores = tile_probs(
            query,
            key_tile,
            value_tile,
            grad_out,
            bias_blk,
            log_total,
            delta,
            key_start,
            crop_lengths,
        )
        dscores_half = dscores.astype(jnp.bfloat16)
        query_sum = query_sum + jnp.einsum(
            "crhjk,crkhd->crjhd",
            dscores_half,
            split_heads(key_tile),
            preferred_element_type=jnp.float32,
        )
        bias_part = lax.dynamic_update_slice_in_dim(
            bias_part, jnp.sum(dscores, axis=1), key_start, 3
        )
        return (probs, dscores_half, query_sum, bias_part)

    query_zero = jnp.zeros(head_shape, jnp.float32)
    bias_zero = jnp.zeros(pair_bias.shape, jnp.float32)

    def carry_update(turn_index, key_tile, value_tile, key_sum, value_sum, query_sum, bias_part):
        probs, dscores_half, query_sum, bias_part = query_update(
            turn_index, key_tile, value_tile, query_sum, bias_part
        )
        probs_half = probs.astype(jnp.bfloat16)
        key_sum = key_sum + jnp.einsum(
            "crhjk,crjhd->crkhd",
            dscores_half,
            split_heads(query),
            preferred_element_type=jnp.float32,
        )
        value_sum = value_sum + jnp.einsum(
            "crhjk,crjhd->crkhd",
            probs_half,
            split_heads(grad_out),
            preferred_element_type=jnp.float32,
        )
        return (key_sum, value_sum, query_sum, bias_part)

    def carry_turn(turn_index, state_tuple):
        key_tile, value_tile, key_sum, value_sum, query_sum, bias_part = state_tuple
        key_sum, value_sum, query_sum, bias_part = carry_update(
            turn_index, key_tile, value_tile, key_sum, value_sum, query_sum, bias_part
        )
        key_tile, value_tile = rotate_tiles(key_tile, value_tile)
        key_sum, value_sum = send_grads(key_sum, value_sum)
        return (key_tile, value_tile, key_sum, value_sum, query_sum, bias_part)

    start_state = (key, value, query_zero, query_zero, query_zero, bias_zero)
    key_tile, value_tile, key_sum, value_sum, query_sum, bias_part = lax.fori_loop(
        0, count - 1, carry_turn, start_state
    )
    key_sum, value_sum, query_sum, bias_part = carry_update(
        count - 1, key_tile, value_tile, key_sum, value_sum, query_sum, bias_part
    )
    key_sum, value_sum = send_grads(key_sum, value_sum)
    grad_bias = lax.psum_scatter(bias_part, "row", scatter_dimension=3, tiled=True)
    flat_shape = query.shape
    grad_query = (query_sum * scale).reshape(flat_shape)
    grad_key = (key_sum * scale).reshape(flat_shape)
    grad_value = value_sum.reshape(flat_shape)
    return (grad_query, grad_key, grad_value, grad_bias)


def solution(mesh):
    return jax.shard_map(
        per_device,
        mesh=mesh,
        in_specs=(
            P(None, "row", "col", None),
            P(None, "row", "col", None),
            P(None, "row", "col", None),
            P(None, "row", "col", None),
            P(None, None, "col", None),
            P(),
        ),
        out_specs=(
            P(None, "row", "col", None),
            P(None, "row", "col", None),
            P(None, "row", "col", None),
            P(None, None, "col", "row"),
        ),
        check_vma=False,
    )
```

profile of v0, /device:TPU:1, one launch (start us, length us, event | category | flops | bytes accessed | tf_op | source)
XLA Modules:
  0.0 1171.1 jit_solution(12137750676632821043)
XLA Ops:
  14.1 287.6 %while.50 = (s32[]{:T(128)}, bf16[2,6,64,128]{2,3,1,0:T(8,128)(2,1)S(1)}, bf16[2,6,64,128]{2,3,1,0:T(8,128)(2,1)S(1)}, f32[2,6,4,64]{3,2,1,0:T(4,128)S(1)}, f32[...) while((s32[]{:T(128)}, ...), condition=%wide.region_4.5_spmd.clone, body=%wide.region_0.4_spmd.clone.sunk | while | flops 26989780 | bytes 6317231 | solution.py:94
  21.3 10.7 collective-permute-done
  32.0 8.4 collective-permute-done.1
  43.7 9.8 collective-permute-done
  53.6 8.4 collective-permute-done.1
  65.3 8.9 collective-permute-done
  74.2 8.4 collective-permute-done.1
  85.9 8.0 collective-permute-done
  93.9 8.4 collective-permute-done.1
  105.6 7.1 collective-permute-done
  112.6 8.4 collective-permute-done.1
  124.3 7.1 collective-permute-done
  131.4 7.5 collective-permute-done.1
  142.2 7.1 collective-permute-done
  149.2 6.6 collective-permute-done.1
  159.1 7.1 collective-permute-done
  166.2 5.6 collective-permute-done.1
  175.1 7.9 collective-permute-done
  183.0 4.8 collective-permute-done.1
  191.1 8.8 collective-permute-done
  199.9 4.2 collective-permute-done.1
  207.4 9.9 collective-permute-done
  217.2 4.2 collective-permute-done.1
  224.7 11.0 collective-permute-done
  235.7 4.2 collective-permute-done.1
  243.1 11.7 collective-permute-done
  254.8 4.6 collective-permute-done.1
  262.7 11.7 collective-permute-done
  274.3 5.7 collective-permute-done.1
  283.2 11.6 collective-permute-done
  294.9 6.8 collective-permute-done.1
  306.1 749.0 %while.51 = (s32[]{:T(128)}, bf16[2,6,64,128]{2,3,1,0:T(8,128)(2,1)}, bf16[2,6,64,128]{2,3,1,0:T(8,128)(2,1)}, f32[2,6,64,4,32]{2,4,3,1,0:T(8,128)}, f32[2,6,64,...) while((s32[]{:T(128)}, ...), condition=%wide.region_10.11_spmd.clone, body=%wide.region_8.10_spmd.clone.sunk | while | flops 65274064 | bytes 13526298 | solution.py:162
  317.8 28.6 %collective-permute-done.2 = bf16[2,6,64,128]{2,3,1,0:T(8,128)(2,1)} collective-permute-done((bf16[2,6,64,128]{2,3,1,0:T(8,128)(2,1)S(1)}, bf16[2,6,64,128]{2,3,1,0:T(8,128)(2,1)}, u32[]{:S(2)}, u32[]{:S(2)}) %collective-permute-start.2) | collective-permute-done | bytes 196640 | tf_op jit(solution)/shard_map/while/body/eval_jaxpr/ppermute | solution.py:13
  346.4 8.3 collective-permute-done.3
  368.1 27.8 %collective-permute-done.2 = bf16[2,6,64,128]{2,3,1,0:T(8,128)(2,1)} collective-permute-done((bf16[2,6,64,128]{2,3,1,0:T(8,128)(2,1)S(1)}, bf16[2,6,64,128]{2,3,1,0:T(8,128)(2,1)}, u32[]{:S(2)}, u32[]{:S(2)}) %collective-permute-start.2) | collective-permute-done | bytes 196640 | tf_op jit(solution)/shard_map/while/body/eval_jaxpr/ppermute | solution.py:13
  396.0 8.3 collective-permute-done.3
  417.0 28.5 %collective-permute-done.2 = bf16[2,6,64,128]{2,3,1,0:T(8,128)(2,1)} collective-permute-done((bf16[2,6,64,128]{2,3,1,0:T(8,128)(2,1)S(1)}, bf16[2,6,64,128]{2,3,1,0:T(8,128)(2,1)}, u32[]{:S(2)}, u32[]{:S(2)}) %collective-permute-start.2) | collective-permute-done | bytes 196640 | tf_op jit(solution)/shard_map/while/body/eval_jaxpr/ppermute | solution.py:13
  445.6 8.4 collective-permute-done.3
  468.1 27.2 %collective-permute-done.2 = bf16[2,6,64,128]{2,3,1,0:T(8,128)(2,1)} collective-permute-done((bf16[2,6,64,128]{2,3,1,0:T(8,128)(2,1)S(1)}, bf16[2,6,64,128]{2,3,1,0:T(8,128)(2,1)}, u32[]{:S(2)}, u32[]{:S(2)}) %collective-permute-start.2) | collective-permute-done | bytes 196640 | tf_op jit(solution)/shard_map/while/body/eval_jaxpr/ppermute | solution.py:13
  495.3 8.4 collective-permute-done.3
  516.6 28.4 %collective-permute-done.2 = bf16[2,6,64,128]{2,3,1,0:T(8,128)(2,1)} collective-permute-done((bf16[2,6,64,128]{2,3,1,0:T(8,128)(2,1)S(1)}, bf16[2,6,64,128]{2,3,1,0:T(8,128)(2,1)}, u32[]{:S(2)}, u32[]{:S(2)}) %collective-permute-start.2) | collective-permute-done | bytes 196640 | tf_op jit(solution)/shard_map/while/body/eval_jaxpr/ppermute | solution.py:13
  545.0 8.4 collective-permute-done.3
  567.6 27.1 %collective-permute-done.2 = bf16[2,6,64,128]{2,3,1,0:T(8,128)(2,1)} collective-permute-done((bf16[2,6,64,128]{2,3,1,0:T(8,128)(2,1)S(1)}, bf16[2,6,64,128]{2,3,1,0:T(8,128)(2,1)}, u32[]{:S(2)}, u32[]{:S(2)}) %collective-permute-start.2) | collective-permute-done | bytes 196640 | tf_op jit(solution)/shard_map/while/body/eval_jaxpr/ppermute | solution.py:13
  594.7 8.4 collective-permute-done.3
  616.0 28.4 %collective-permute-done.2 = bf16[2,6,64,128]{2,3,1,0:T(8,128)(2,1)} collective-permute-done((bf16[2,6,64,128]{2,3,1,0:T(8,128)(2,1)S(1)}, bf16[2,6,64,128]{2,3,1,0:T(8,128)(2,1)}, u32[]{:S(2)}, u32[]{:S(2)}) %collective-permute-start.2) | collective-permute-done | bytes 196640 | tf_op jit(solution)/shard_map/while/body/eval_jaxpr/ppermute | solution.py:13
  644.4 8.4 collective-permute-done.3
  667.0 27.5 %collective-permute-done.2 = bf16[2,6,64,128]{2,3,1,0:T(8,128)(2,1)} collective-permute-done((bf16[2,6,64,128]{2,3,1,0:T(8,128)(2,1)S(1)}, bf16[2,6,64,128]{2,3,1,0:T(8,128)(2,1)}, u32[]{:S(2)}, u32[]{:S(2)}) %collective-permute-start.2) | collective-permute-done | bytes 196640 | tf_op jit(solution)/shard_map/while/body/eval_jaxpr/ppermute | solution.py:13
  694.5 8.0 collective-permute-done.3
  715.4 29.7 %collective-permute-done.2 = bf16[2,6,64,128]{2,3,1,0:T(8,128)(2,1)} collective-permute-done((bf16[2,6,64,128]{2,3,1,0:T(8,128)(2,1)S(1)}, bf16[2,6,64,128]{2,3,1,0:T(8,128)(2,1)}, u32[]{:S(2)}, u32[]{:S(2)}) %collective-permute-start.2) | collective-permute-done | bytes 196640 | tf_op jit(solution)/shard_map/while/body/eval_jaxpr/ppermute | solution.py:13
  745.1 7.2 collective-permute-done.3
  766.4 29.2 %collective-permute-done.2 = bf16[2,6,64,128]{2,3,1,0:T(8,128)(2,1)} collective-permute-done((bf16[2,6,64,128]{2,3,1,0:T(8,128)(2,1)S(1)}, bf16[2,6,64,128]{2,3,1,0:T(8,128)(2,1)}, u32[]{:S(2)}, u32[]{:S(2)}) %collective-permute-start.2) | collective-permute-done | bytes 196640 | tf_op jit(solution)/shard_map/while/body/eval_jaxpr/ppermute | solution.py:13
  795.6 6.3 collective-permute-done.3
  814.8 31.4 %collective-permute-done.2 = bf16[2,6,64,128]{2,3,1,0:T(8,128)(2,1)} collective-permute-done((bf16[2,6,64,128]{2,3,1,0:T(8,128)(2,1)S(1)}, bf16[2,6,64,128]{2,3,1,0:T(8,128)(2,1)}, u32[]{:S(2)}, u32[]{:S(2)}) %collective-permute-start.2) | collective-permute-done | bytes 196640 | tf_op jit(solution)/shard_map/while/body/eval_jaxpr/ppermute | solution.py:13
  846.2 5.5 collective-permute-done.3
  865.8 31.0 %collective-permute-done.2 = bf16[2,6,64,128]{2,3,1,0:T(8,128)(2,1)} collective-permute-done((bf16[2,6,64,128]{2,3,1,0:T(8,128)(2,1)S(1)}, bf16[2,6,64,128]{2,3,1,0:T(8,128)(2,1)}, u32[]{:S(2)}, u32[]{:S(2)}) %collective-permute-start.2) | collective-permute-done | bytes 196640 | tf_op jit(solution)/shard_map/while/body/eval_jaxpr/ppermute | solution.py:13
  896.7 4.6 collective-permute-done.3
  914.2 33.1 %collective-permute-done.2 = bf16[2,6,64,128]{2,3,1,0:T(8,128)(2,1)} collective-permute-done((bf16[2,6,64,128]{2,3,1,0:T(8,128)(2,1)S(1)}, bf16[2,6,64,128]{2,3,1,0:T(8,128)(2,1)}, u32[]{:S(2)}, u32[]{:S(2)}) %collective-permute-start.2) | collective-permute-done | bytes 196640 | tf_op jit(solution)/shard_map/while/body/eval_jaxpr/ppermute | solution.py:13
  965.6 32.9 %collective-permute-done.2 = bf16[2,6,64,128]{2,3,1,0:T(8,128)(2,1)} collective-permute-done((bf16[2,6,64,128]{2,3,1,0:T(8,128)(2,1)S(1)}, bf16[2,6,64,128]{2,3,1,0:T(8,128)(2,1)}, u32[]{:S(2)}, u32[]{:S(2)}) %collective-permute-start.2) | collective-permute-done | bytes 196640 | tf_op jit(solution)/shard_map/while/body/eval_jaxpr/ppermute | solution.py:13
  1015.6 35.3 %collective-permute-done.2 = bf16[2,6,64,128]{2,3,1,0:T(8,128)(2,1)} collective-permute-done((bf16[2,6,64,128]{2,3,1,0:T(8,128)(2,1)S(1)}, bf16[2,6,64,128]{2,3,1,0:T(8,128)(2,1)}, u32[]{:S(2)}, u32[]{:S(2)}) %collective-permute-start.2) | collective-permute-done | bytes 196640 | tf_op jit(solution)/shard_map/while/body/eval_jaxpr/ppermute | solution.py:13
  1062.1 4.8 copy.72
  1066.9 5.6 reshape.236
  1078.7 12.9 %collective-permute-done.6 = f32[2,6,64,4,32]{2,4,3,1,0:T(8,128)} collective-permute-done((f32[2,6,64,4,32]{2,4,3,1,0:T(8,128)}, f32[2,6,64,4,32]{2,4,3,1,0:T(8,128)}, u32[]{:S(2)}, u32[]{:S(2)}) %collective-permute-start.6) | collective-permute-done | bytes 393248 | tf_op jit(solution)/shard_map/ppermute | solution.py:13
  1093.8 6.1 collective-permute-done.7
  1100.9 61.5 %reduce-scatter.4.cloned.1.call-done = f32[64,512]{1,0:T(8,128)} async-done(((f32[1024,512]{1,0:T(8,128)}), f32[64,512]{1,0:T(8,128)}) %reduce-scatter.4.cloned.1.call-update) | async-done | bytes 131088
  (538 shorter events, 292.6 us)
Async XLA Ops:
  7.2 1155.2 %reduce-scatter.4.cloned.1.call-start = ((), (), s32[]{:S(2)}) async-start(), calls=%async_computation.1 | async-start | bytes 2228224
  16.7 23.8 %collective-permute-start.1 = (bf16[2,6,64,128]{2,3,1,0:T(8,128)(2,1)S(1)}, bf16[2,6,64,128]{2,3,1,0:T(8,128)(2,1)S(1)}, u32[]{:S(2)}, u32[]{:S(2)}) collective-permute-start(bf16[2,6,64,128]{2,3,1,0:T(8,128)(2,1)S(1)} %copy.86), channel_id=1, source_target_pairs={{15,0},{0,1},{1,2},{2,3},{3,4},{4,5},{5,6},{6,7},{7,8},{8,9},{9,10... | collective-permute-start | bytes 589832 | tf_op jit(solution)/shard_map/while/body/eval_jaxpr/ppermute | solution.py:13
  280.1 21.5 %collective-permute-start.1 = (bf16[2,6,64,128]{2,3,1,0:T(8,128)(2,1)S(1)}, bf16[2,6,64,128]{2,3,1,0:T(8,128)(2,1)S(1)}, u32[]{:S(2)}, u32[]{:S(2)}) collective-permute-start(bf16[2,6,64,128]{2,3,1,0:T(8,128)(2,1)S(1)} %copy.86), channel_id=1, source_target_pairs={{15,0},{0,1},{1,2},{2,3},{3,4},{4,5},{5,6},{6,7},{7,8},{8,9},{9,10... | collective-permute-start | bytes 589832 | tf_op jit(solution)/shard_map/while/body/eval_jaxpr/ppermute | solution.py:13
  313.2 41.5 %collective-permute-start.4 = (f32[2,6,64,4,32]{2,4,3,1,0:T(8,128)}, f32[2,6,64,4,32]{2,4,3,1,0:T(8,128)}, u32[]{:S(2)}, u32[]{:S(2)}) collective-permute-start(f32[2,6,64,4,32]{2,4,3,1,0:T(8,128)} %fusion.92), channel_id=1, source_target_pairs={{15,0},{0,1},{1,2},{2,3},{3,4},{4,5},{5,6},{6,7},{7,8},{8,9},{9,10... | collective-permute-start | bytes 1179656 | tf_op jit(solution)/shard_map/while/body/eval_jaxpr/ppermute | solution.py:13
  314.4 40.3 %collective-permute-start.5 = (f32[2,6,64,4,32]{2,4,3,1,0:T(8,128)}, f32[2,6,64,4,32]{2,4,3,1,0:T(8,128)S(1)}, u32[]{:S(2)}, u32[]{:S(2)}) collective-permute-start(f32[2,6,64,4,32]{2,4,3,1,0:T(8,128)} %fusion.93), channel_id=1, source_target_pairs={{15,0},{0,1},{1,2},{2,3},{3,4},{4,5},{5,6},{6,7},{7,8},{8,9},{9,10... | collective-permute-start | bytes 1179656 | tf_op jit(solution)/shard_map/while/body/eval_jaxpr/ppermute | solution.py:13
  314.4 32.0 %collective-permute-start.2 = (bf16[2,6,64,128]{2,3,1,0:T(8,128)(2,1)S(1)}, bf16[2,6,64,128]{2,3,1,0:T(8,128)(2,1)}, u32[]{:S(2)}, u32[]{:S(2)}) collective-permute-start(bf16[2,6,64,128]{2,3,1,0:T(8,128)(2,1)S(1)} %copy.104), channel_id=1, source_target_pairs={{15,0},{0,1},{1,2},{2,3},{3,4},{4,5},{5,6},{6,7},{7,8},{8,9},{9,10... | collective-permute-start | bytes 589832 | tf_op jit(solution)/shard_map/while/body/eval_jaxpr/ppermute | solution.py:13
  314.4 40.3 %collective-permute-start.3 = (bf16[2,6,64,128]{2,3,1,0:T(8,128)(2,1)S(1)}, bf16[2,6,64,128]{2,3,1,0:T(8,128)(2,1)}, u32[]{:S(2)}, u32[]{:S(2)}) collective-permute-start(bf16[2,6,64,128]{2,3,1,0:T(8,128)(2,1)S(1)} %copy.105), channel_id=1, source_target_pairs={{15,0},{0,1},{1,2},{2,3},{3,4},{4,5},{5,6},{6,7},{7,8},{8,9},{9,10... | collective-permute-start | bytes 589832 | tf_op jit(solution)/shard_map/while/body/eval_jaxpr/ppermute | solution.py:13
  361.8 42.5 %collective-permute-start.4 = (f32[2,6,64,4,32]{2,4,3,1,0:T(8,128)}, f32[2,6,64,4,32]{2,4,3,1,0:T(8,128)}, u32[]{:S(2)}, u32[]{:S(2)}) collective-permute-start(f32[2,6,64,4,32]{2,4,3,1,0:T(8,128)} %fusion.92), channel_id=1, source_target_pairs={{15,0},{0,1},{1,2},{2,3},{3,4},{4,5},{5,6},{6,7},{7,8},{8,9},{9,10... | collective-permute-start | bytes 1179656 | tf_op jit(solution)/shard_map/while/body/eval_jaxpr/ppermute | solution.py:13
  363.1 41.2 %collective-permute-start.5 = (f32[2,6,64,4,32]{2,4,3,1,0:T(8,128)}, f32[2,6,64,4,32]{2,4,3,1,0:T(8,128)S(1)}, u32[]{:S(2)}, u32[]{:S(2)}) collective-permute-start(f32[2,6,64,4,32]{2,4,3,1,0:T(8,128)} %fusion.93), channel_id=1, source_target_pairs={{15,0},{0,1},{1,2},{2,3},{3,4},{4,5},{5,6},{6,7},{7,8},{8,9},{9,10... | collective-permute-start | bytes 1179656 | tf_op jit(solution)/shard_map/while/body/eval_jaxpr/ppermute | solution.py:13
  363.1 32.9 %collective-permute-start.2 = (bf16[2,6,64,128]{2,3,1,0:T(8,128)(2,1)S(1)}, bf16[2,6,64,128]{2,3,1,0:T(8,128)(2,1)}, u32[]{:S(2)}, u32[]{:S(2)}) collective-permute-start(bf16[2,6,64,128]{2,3,1,0:T(8,128)(2,1)S(1)} %copy.104), channel_id=1, source_target_pairs={{15,0},{0,1},{1,2},{2,3},{3,4},{4,5},{5,6},{6,7},{7,8},{8,9},{9,10... | collective-permute-start | bytes 589832 | tf_op jit(solution)/shard_map/while/body/eval_jaxpr/ppermute | solution.py:13
  363.1 41.2 %collective-permute-start.3 = (bf16[2,6,64,128]{2,3,1,0:T(8,128)(2,1)S(1)}, bf16[2,6,64,128]{2,3,1,0:T(8,128)(2,1)}, u32[]{:S(2)}, u32[]{:S(2)}) collective-permute-start(bf16[2,6,64,128]{2,3,1,0:T(8,128)(2,1)S(1)} %copy.105), channel_id=1, source_target_pairs={{15,0},{0,1},{1,2},{2,3},{3,4},{4,5},{5,6},{6,7},{7,8},{8,9},{9,10... | collective-permute-start | bytes 589832 | tf_op jit(solution)/shard_map/while/body/eval_jaxpr/ppermute | solution.py:13
  411.4 42.6 %collective-permute-start.4 = (f32[2,6,64,4,32]{2,4,3,1,0:T(8,128)}, f32[2,6,64,4,32]{2,4,3,1,0:T(8,128)}, u32[]{:S(2)}, u32[]{:S(2)}) collective-permute-start(f32[2,6,64,4,32]{2,4,3,1,0:T(8,128)} %fusion.92), channel_id=1, source_target_pairs={{15,0},{0,1},{1,2},{2,3},{3,4},{4,5},{5,6},{6,7},{7,8},{8,9},{9,10... | collective-permute-start | bytes 1179656 | tf_op jit(solution)/shard_map/while/body/eval_jaxpr/ppermute | solution.py:13
  412.7 41.4 %collective-permute-start.5 = (f32[2,6,64,4,32]{2,4,3,1,0:T(8,128)}, f32[2,6,64,4,32]{2,4,3,1,0:T(8,128)S(1)}, u32[]{:S(2)}, u32[]{:S(2)}) collective-permute-start(f32[2,6,64,4,32]{2,4,3,1,0:T(8,128)} %fusion.93), channel_id=1, source_target_pairs={{15,0},{0,1},{1,2},{2,3},{3,4},{4,5},{5,6},{6,7},{7,8},{8,9},{9,10... | collective-permute-start | bytes 1179656 | tf_op jit(solution)/shard_map/while/body/eval_jaxpr/ppermute | solution.py:13
  412.7 32.9 %collective-permute-start.2 = (bf16[2,6,64,128]{2,3,1,0:T(8,128)(2,1)S(1)}, bf16[2,6,64,128]{2,3,1,0:T(8,128)(2,1)}, u32[]{:S(2)}, u32[]{:S(2)}) collective-permute-start(bf16[2,6,64,128]{2,3,1,0:T(8,128)(2,1)S(1)} %copy.104), channel_id=1, source_target_pairs={{15,0},{0,1},{1,2},{2,3},{3,4},{4,5},{5,6},{6,7},{7,8},{8,9},{9,10... | collective-permute-start | bytes 589832 | tf_op jit(solution)/shard_map/while/body/eval_jaxpr/ppermute | solution.py:13
  412.7 41.3 %collective-permute-start.3 = (bf16[2,6,64,128]{2,3,1,0:T(8,128)(2,1)S(1)}, bf16[2,6,64,128]{2,3,1,0:T(8,128)(2,1)}, u32[]{:S(2)}, u32[]{:S(2)}) collective-permute-start(bf16[2,6,64,128]{2,3,1,0:T(8,128)(2,1)S(1)} %copy.105), channel_id=1, source_target_pairs={{15,0},{0,1},{1,2},{2,3},{3,4},{4,5},{5,6},{6,7},{7,8},{8,9},{9,10... | collective-permute-start | bytes 589832 | tf_op jit(solution)/shard_map/while/body/eval_jaxpr/ppermute | solution.py:13
  461.1 42.6 %collective-permute-start.4 = (f32[2,6,64,4,32]{2,4,3,1,0:T(8,128)}, f32[2,6,64,4,32]{2,4,3,1,0:T(8,128)}, u32[]{:S(2)}, u32[]{:S(2)}) collective-permute-start(f32[2,6,64,4,32]{2,4,3,1,0:T(8,128)} %fusion.92), channel_id=1, source_target_pairs={{15,0},{0,1},{1,2},{2,3},{3,4},{4,5},{5,6},{6,7},{7,8},{8,9},{9,10... | collective-permute-start | bytes 1179656 | tf_op jit(solution)/shard_map/while/body/eval_jaxpr/ppermute | solution.py:13
  462.4 41.4 %collective-permute-start.5 = (f32[2,6,64,4,32]{2,4,3,1,0:T(8,128)}, f32[2,6,64,4,32]{2,4,3,1,0:T(8,128)S(1)}, u32[]{:S(2)}, u32[]{:S(2)}) collective-permute-start(f32[2,6,64,4,32]{2,4,3,1,0:T(8,128)} %fusion.93), channel_id=1, source_target_pairs={{15,0},{0,1},{1,2},{2,3},{3,4},{4,5},{5,6},{6,7},{7,8},{8,9},{9,10... | collective-permute-start | bytes 1179656 | tf_op jit(solution)/shard_map/while/body/eval_jaxpr/ppermute | solution.py:13
  462.4 32.9 %collective-permute-start.2 = (bf16[2,6,64,128]{2,3,1,0:T(8,128)(2,1)S(1)}, bf16[2,6,64,128]{2,3,1,0:T(8,128)(2,1)}, u32[]{:S(2)}, u32[]{:S(2)}) collective-permute-start(bf16[2,6,64,128]{2,3,1,0:T(8,128)(2,1)S(1)} %copy.104), channel_id=1, source_target_pairs={{15,0},{0,1},{1,2},{2,3},{3,4},{4,5},{5,6},{6,7},{7,8},{8,9},{9,10... | collective-permute-start | bytes 589832 | tf_op jit(solution)/shard_map/while/body/eval_jaxpr/ppermute | solution.py:13
  462.4 41.3 %collective-permute-start.3 = (bf16[2,6,64,128]{2,3,1,0:T(8,128)(2,1)S(1)}, bf16[2,6,64,128]{2,3,1,0:T(8,128)(2,1)}, u32[]{:S(2)}, u32[]{:S(2)}) collective-permute-start(bf16[2,6,64,128]{2,3,1,0:T(8,128)(2,1)S(1)} %copy.105), channel_id=1, source_target_pairs={{15,0},{0,1},{1,2},{2,3},{3,4},{4,5},{5,6},{6,7},{7,8},{8,9},{9,10... | collective-permute-start | bytes 589832 | tf_op jit(solution)/shard_map/while/body/eval_jaxpr/ppermute | solution.py:13
  510.8 42.6 %collective-permute-start.4 = (f32[2,6,64,4,32]{2,4,3,1,0:T(8,128)}, f32[2,6,64,4,32]{2,4,3,1,0:T(8,128)}, u32[]{:S(2)}, u32[]{:S(2)}) collective-permute-start(f32[2,6,64,4,32]{2,4,3,1,0:T(8,128)} %fusion.92), channel_id=1, source_target_pairs={{15,0},{0,1},{1,2},{2,3},{3,4},{4,5},{5,6},{6,7},{7,8},{8,9},{9,10... | collective-permute-start | bytes 1179656 | tf_op jit(solution)/shard_map/while/body/eval_jaxpr/ppermute | solution.py:13
  512.1 41.3 %collective-permute-start.5 = (f32[2,6,64,4,32]{2,4,3,1,0:T(8,128)}, f32[2,6,64,4,32]{2,4,3,1,0:T(8,128)S(1)}, u32[]{:S(2)}, u32[]{:S(2)}) collective-permute-start(f32[2,6,64,4,32]{2,4,3,1,0:T(8,128)} %fusion.93), channel_id=1, source_target_pairs={{15,0},{0,1},{1,2},{2,3},{3,4},{4,5},{5,6},{6,7},{7,8},{8,9},{9,10... | collective-permute-start | bytes 1179656 | tf_op jit(solution)/shard_map/while/body/eval_jaxpr/ppermute | solution.py:13
  512.1 32.9 %collective-permute-start.2 = (bf16[2,6,64,128]{2,3,1,0:T(8,128)(2,1)S(1)}, bf16[2,6,64,128]{2,3,1,0:T(8,128)(2,1)}, u32[]{:S(2)}, u32[]{:S(2)}) collective-permute-start(bf16[2,6,64,128]{2,3,1,0:T(8,128)(2,1)S(1)} %copy.104), channel_id=1, source_target_pairs={{15,0},{0,1},{1,2},{2,3},{3,4},{4,5},{5,6},{6,7},{7,8},{8,9},{9,10... | collective-permute-start | bytes 589832 | tf_op jit(solution)/shard_map/while/body/eval_jaxpr/ppermute | solution.py:13
  512.1 41.3 %collective-permute-start.3 = (bf16[2,6,64,128]{2,3,1,0:T(8,128)(2,1)S(1)}, bf16[2,6,64,128]{2,3,1,0:T(8,128)(2,1)}, u32[]{:S(2)}, u32[]{:S(2)}) collective-permute-start(bf16[2,6,64,128]{2,3,1,0:T(8,128)(2,1)S(1)} %copy.105), channel_id=1, source_target_pairs={{15,0},{0,1},{1,2},{2,3},{3,4},{4,5},{5,6},{6,7},{7,8},{8,9},{9,10... | collective-permute-start | bytes 589832 | tf_op jit(solution)/shard_map/while/body/eval_jaxpr/ppermute | solution.py:13
  560.5 42.6 %collective-permute-start.4 = (f32[2,6,64,4,32]{2,4,3,1,0:T(8,128)}, f32[2,6,64,4,32]{2,4,3,1,0:T(8,128)}, u32[]{:S(2)}, u32[]{:S(2)}) collective-permute-start(f32[2,6,64,4,32]{2,4,3,1,0:T(8,128)} %fusion.92), channel_id=1, source_target_pairs={{15,0},{0,1},{1,2},{2,3},{3,4},{4,5},{5,6},{6,7},{7,8},{8,9},{9,10... | collective-permute-start | bytes 1179656 | tf_op jit(solution)/shard_map/while/body/eval_jaxpr/ppermute | solution.py:13
  561.8 41.4 %collective-permute-start.5 = (f32[2,6,64,4,32]{2,4,3,1,0:T(8,128)}, f32[2,6,64,4,32]{2,4,3,1,0:T(8,128)S(1)}, u32[]{:S(2)}, u32[]{:S(2)}) collective-permute-start(f32[2,6,64,4,32]{2,4,3,1,0:T(8,128)} %fusion.93), channel_id=1, source_target_pairs={{15,0},{0,1},{1,2},{2,3},{3,4},{4,5},{5,6},{6,7},{7,8},{8,9},{9,10... | collective-permute-start | bytes 1179656 | tf_op jit(solution)/shard_map/while/body/eval_jaxpr/ppermute | solution.py:13
  561.8 32.9 %collective-permute-start.2 = (bf16[2,6,64,128]{2,3,1,0:T(8,128)(2,1)S(1)}, bf16[2,6,64,128]{2,3,1,0:T(8,128)(2,1)}, u32[]{:S(2)}, u32[]{:S(2)}) collective-permute-start(bf16[2,6,64,128]{2,3,1,0:T(8,128)(2,1)S(1)} %copy.104), channel_id=1, source_target_pairs={{15,0},{0,1},{1,2},{2,3},{3,4},{4,5},{5,6},{6,7},{7,8},{8,9},{9,10... | collective-permute-start | bytes 589832 | tf_op jit(solution)/shard_map/while/body/eval_jaxpr/ppermute | solution.py:13
  561.8 41.3 %collective-permute-start.3 = (bf16[2,6,64,128]{2,3,1,0:T(8,128)(2,1)S(1)}, bf16[2,6,64,128]{2,3,1,0:T(8,128)(2,1)}, u32[]{:S(2)}, u32[]{:S(2)}) collective-permute-start(bf16[2,6,64,128]{2,3,1,0:T(8,128)(2,1)S(1)} %copy.105), channel_id=1, source_target_pairs={{15,0},{0,1},{1,2},{2,3},{3,4},{4,5},{5,6},{6,7},{7,8},{8,9},{9,10... | collective-permute-start | bytes 589832 | tf_op jit(solution)/shard_map/while/body/eval_jaxpr/ppermute | solution.py:13
  610.3 42.6 %collective-permute-start.4 = (f32[2,6,64,4,32]{2,4,3,1,0:T(8,128)}, f32[2,6,64,4,32]{2,4,3,1,0:T(8,128)}, u32[]{:S(2)}, u32[]{:S(2)}) collective-permute-start(f32[2,6,64,4,32]{2,4,3,1,0:T(8,128)} %fusion.92), channel_id=1, source_target_pairs={{15,0},{0,1},{1,2},{2,3},{3,4},{4,5},{5,6},{6,7},{7,8},{8,9},{9,10... | collective-permute-start | bytes 1179656 | tf_op jit(solution)/shard_map/while/body/eval_jaxpr/ppermute | solution.py:13
  611.5 41.4 %collective-permute-start.5 = (f32[2,6,64,4,32]{2,4,3,1,0:T(8,128)}, f32[2,6,64,4,32]{2,4,3,1,0:T(8,128)S(1)}, u32[]{:S(2)}, u32[]{:S(2)}) collective-permute-start(f32[2,6,64,4,32]{2,4,3,1,0:T(8,128)} %fusion.93), channel_id=1, source_target_pairs={{15,0},{0,1},{1,2},{2,3},{3,4},{4,5},{5,6},{6,7},{7,8},{8,9},{9,10... | collective-permute-start | bytes 1179656 | tf_op jit(solution)/shard_map/while/body/eval_jaxpr/ppermute | solution.py:13
  611.5 32.9 %collective-permute-start.2 = (bf16[2,6,64,128]{2,3,1,0:T(8,128)(2,1)S(1)}, bf16[2,6,64,128]{2,3,1,0:T(8,128)(2,1)}, u32[]{:S(2)}, u32[]{:S(2)}) collective-permute-start(bf16[2,6,64,128]{2,3,1,0:T(8,128)(2,1)S(1)} %copy.104), channel_id=1, source_target_pairs={{15,0},{0,1},{1,2},{2,3},{3,4},{4,5},{5,6},{6,7},{7,8},{8,9},{9,10... | collective-permute-start | bytes 589832 | tf_op jit(solution)/shard_map/while/body/eval_jaxpr/ppermute | solution.py:13
  611.5 41.3 %collective-permute-start.3 = (bf16[2,6,64,128]{2,3,1,0:T(8,128)(2,1)S(1)}, bf16[2,6,64,128]{2,3,1,0:T(8,128)(2,1)}, u32[]{:S(2)}, u32[]{:S(2)}) collective-permute-start(bf16[2,6,64,128]{2,3,1,0:T(8,128)(2,1)S(1)} %copy.105), channel_id=1, source_target_pairs={{15,0},{0,1},{1,2},{2,3},{3,4},{4,5},{5,6},{6,7},{7,8},{8,9},{9,10... | collective-permute-start | bytes 589832 | tf_op jit(solution)/shard_map/while/body/eval_jaxpr/ppermute | solution.py:13
  660.0 42.6 %collective-permute-start.4 = (f32[2,6,64,4,32]{2,4,3,1,0:T(8,128)}, f32[2,6,64,4,32]{2,4,3,1,0:T(8,128)}, u32[]{:S(2)}, u32[]{:S(2)}) collective-permute-start(f32[2,6,64,4,32]{2,4,3,1,0:T(8,128)} %fusion.92), channel_id=1, source_target_pairs={{15,0},{0,1},{1,2},{2,3},{3,4},{4,5},{5,6},{6,7},{7,8},{8,9},{9,10... | collective-permute-start | bytes 1179656 | tf_op jit(solution)/shard_map/while/body/eval_jaxpr/ppermute | solution.py:13
  661.2 41.4 %collective-permute-start.5 = (f32[2,6,64,4,32]{2,4,3,1,0:T(8,128)}, f32[2,6,64,4,32]{2,4,3,1,0:T(8,128)S(1)}, u32[]{:S(2)}, u32[]{:S(2)}) collective-permute-start(f32[2,6,64,4,32]{2,4,3,1,0:T(8,128)} %fusion.93), channel_id=1, source_target_pairs={{15,0},{0,1},{1,2},{2,3},{3,4},{4,5},{5,6},{6,7},{7,8},{8,9},{9,10... | collective-permute-start | bytes 1179656 | tf_op jit(solution)/shard_map/while/body/eval_jaxpr/ppermute | solution.py:13
  661.2 33.3 %collective-permute-start.2 = (bf16[2,6,64,128]{2,3,1,0:T(8,128)(2,1)S(1)}, bf16[2,6,64,128]{2,3,1,0:T(8,128)(2,1)}, u32[]{:S(2)}, u32[]{:S(2)}) collective-permute-start(bf16[2,6,64,128]{2,3,1,0:T(8,128)(2,1)S(1)} %copy.104), channel_id=1, source_target_pairs={{15,0},{0,1},{1,2},{2,3},{3,4},{4,5},{5,6},{6,7},{7,8},{8,9},{9,10... | collective-permute-start | bytes 589832 | tf_op jit(solution)/shard_map/while/body/eval_jaxpr/ppermute | solution.py:13
  661.2 41.3 %collective-permute-start.3 = (bf16[2,6,64,128]{2,3,1,0:T(8,128)(2,1)S(1)}, bf16[2,6,64,128]{2,3,1,0:T(8,128)(2,1)}, u32[]{:S(2)}, u32[]{:S(2)}) collective-permute-start(bf16[2,6,64,128]{2,3,1,0:T(8,128)(2,1)S(1)} %copy.105), channel_id=1, source_target_pairs={{15,0},{0,1},{1,2},{2,3},{3,4},{4,5},{5,6},{6,7},{7,8},{8,9},{9,10... | collective-permute-start | bytes 589832 | tf_op jit(solution)/shard_map/while/body/eval_jaxpr/ppermute | solution.py:13
  709.7 42.6 %collective-permute-start.4 = (f32[2,6,64,4,32]{2,4,3,1,0:T(8,128)}, f32[2,6,64,4,32]{2,4,3,1,0:T(8,128)}, u32[]{:S(2)}, u32[]{:S(2)}) collective-permute-start(f32[2,6,64,4,32]{2,4,3,1,0:T(8,128)} %fusion.92), channel_id=1, source_target_pairs={{15,0},{0,1},{1,2},{2,3},{3,4},{4,5},{5,6},{6,7},{7,8},{8,9},{9,10... | collective-permute-start | bytes 1179656 | tf_op jit(solution)/shard_map/while/body/eval_jaxpr/ppermute | solution.py:13
  710.9 41.4 %collective-permute-start.5 = (f32[2,6,64,4,32]{2,4,3,1,0:T(8,128)}, f32[2,6,64,4,32]{2,4,3,1,0:T(8,128)S(1)}, u32[]{:S(2)}, u32[]{:S(2)}) collective-permute-start(f32[2,6,64,4,32]{2,4,3,1,0:T(8,128)} %fusion.93), channel_id=1, source_target_pairs={{15,0},{0,1},{1,2},{2,3},{3,4},{4,5},{5,6},{6,7},{7,8},{8,9},{9,10... | collective-permute-start | bytes 1179656 | tf_op jit(solution)/shard_map/while/body/eval_jaxpr/ppermute | solution.py:13
  710.9 34.2 %collective-permute-start.2 = (bf16[2,6,64,128]{2,3,1,0:T(8,128)(2,1)S(1)}, bf16[2,6,64,128]{2,3,1,0:T(8,128)(2,1)}, u32[]{:S(2)}, u32[]{:S(2)}) collective-permute-start(bf16[2,6,64,128]{2,3,1,0:T(8,128)(2,1)S(1)} %copy.104), channel_id=1, source_target_pairs={{15,0},{0,1},{1,2},{2,3},{3,4},{4,5},{5,6},{6,7},{7,8},{8,9},{9,10... | collective-permute-start | bytes 589832 | tf_op jit(solution)/shard_map/while/body/eval_jaxpr/ppermute | solution.py:13
  710.9 41.3 %collective-permute-start.3 = (bf16[2,6,64,128]{2,3,1,0:T(8,128)(2,1)S(1)}, bf16[2,6,64,128]{2,3,1,0:T(8,128)(2,1)}, u32[]{:S(2)}, u32[]{:S(2)}) collective-permute-start(bf16[2,6,64,128]{2,3,1,0:T(8,128)(2,1)S(1)} %copy.105), channel_id=1, source_target_pairs={{15,0},{0,1},{1,2},{2,3},{3,4},{4,5},{5,6},{6,7},{7,8},{8,9},{9,10... | collective-permute-start | bytes 589832 | tf_op jit(solution)/shard_map/while/body/eval_jaxpr/ppermute | solution.py:13
  759.4 42.6 %collective-permute-start.4 = (f32[2,6,64,4,32]{2,4,3,1,0:T(8,128)}, f32[2,6,64,4,32]{2,4,3,1,0:T(8,128)}, u32[]{:S(2)}, u32[]{:S(2)}) collective-permute-start(f32[2,6,64,4,32]{2,4,3,1,0:T(8,128)} %fusion.92), channel_id=1, source_target_pairs={{15,0},{0,1},{1,2},{2,3},{3,4},{4,5},{5,6},{6,7},{7,8},{8,9},{9,10... | collective-permute-start | bytes 1179656 | tf_op jit(solution)/shard_map/while/body/eval_jaxpr/ppermute | solution.py:13
  760.6 41.4 %collective-permute-start.5 = (f32[2,6,64,4,32]{2,4,3,1,0:T(8,128)}, f32[2,6,64,4,32]{2,4,3,1,0:T(8,128)S(1)}, u32[]{:S(2)}, u32[]{:S(2)}) collective-permute-start(f32[2,6,64,4,32]{2,4,3,1,0:T(8,128)} %fusion.93), channel_id=1, source_target_pairs={{15,0},{0,1},{1,2},{2,3},{3,4},{4,5},{5,6},{6,7},{7,8},{8,9},{9,10... | collective-permute-start | bytes 1179656 | tf_op jit(solution)/shard_map/while/body/eval_jaxpr/ppermute | solution.py:13
  760.6 35.0 %collective-permute-start.2 = (bf16[2,6,64,128]{2,3,1,0:T(8,128)(2,1)S(1)}, bf16[2,6,64,128]{2,3,1,0:T(8,128)(2,1)}, u32[]{:S(2)}, u32[]{:S(2)}) collective-permute-start(bf16[2,6,64,128]{2,3,1,0:T(8,128)(2,1)S(1)} %copy.104), channel_id=1, source_target_pairs={{15,0},{0,1},{1,2},{2,3},{3,4},{4,5},{5,6},{6,7},{7,8},{8,9},{9,10... | collective-permute-start | bytes 589832 | tf_op jit(solution)/shard_map/while/body/eval_jaxpr/ppermute | solution.py:13
  760.6 41.3 %collective-permute-start.3 = (bf16[2,6,64,128]{2,3,1,0:T(8,128)(2,1)S(1)}, bf16[2,6,64,128]{2,3,1,0:T(8,128)(2,1)}, u32[]{:S(2)}, u32[]{:S(2)}) collective-permute-start(bf16[2,6,64,128]{2,3,1,0:T(8,128)(2,1)S(1)} %copy.105), channel_id=1, source_target_pairs={{15,0},{0,1},{1,2},{2,3},{3,4},{4,5},{5,6},{6,7},{7,8},{8,9},{9,10... | collective-permute-start | bytes 589832 | tf_op jit(solution)/shard_map/while/body/eval_jaxpr/ppermute | solution.py:13
  809.1 42.6 %collective-permute-start.4 = (f32[2,6,64,4,32]{2,4,3,1,0:T(8,128)}, f32[2,6,64,4,32]{2,4,3,1,0:T(8,128)}, u32[]{:S(2)}, u32[]{:S(2)}) collective-permute-start(f32[2,6,64,4,32]{2,4,3,1,0:T(8,128)} %fusion.92), channel_id=1, source_target_pairs={{15,0},{0,1},{1,2},{2,3},{3,4},{4,5},{5,6},{6,7},{7,8},{8,9},{9,10... | collective-permute-start | bytes 1179656 | tf_op jit(solution)/shard_map/while/body/eval_jaxpr/ppermute | solution.py:13
  810.3 41.4 %collective-permute-start.5 = (f32[2,6,64,4,32]{2,4,3,1,0:T(8,128)}, f32[2,6,64,4,32]{2,4,3,1,0:T(8,128)S(1)}, u32[]{:S(2)}, u32[]{:S(2)}) collective-permute-start(f32[2,6,64,4,32]{2,4,3,1,0:T(8,128)} %fusion.93), channel_id=1, source_target_pairs={{15,0},{0,1},{1,2},{2,3},{3,4},{4,5},{5,6},{6,7},{7,8},{8,9},{9,10... | collective-permute-start | bytes 1179656 | tf_op jit(solution)/shard_map/while/body/eval_jaxpr/ppermute | solution.py:13
  810.3 35.9 %collective-permute-start.2 = (bf16[2,6,64,128]{2,3,1,0:T(8,128)(2,1)S(1)}, bf16[2,6,64,128]{2,3,1,0:T(8,128)(2,1)}, u32[]{:S(2)}, u32[]{:S(2)}) collective-permute-start(bf16[2,6,64,128]{2,3,1,0:T(8,128)(2,1)S(1)} %copy.104), channel_id=1, source_target_pairs={{15,0},{0,1},{1,2},{2,3},{3,4},{4,5},{5,6},{6,7},{7,8},{8,9},{9,10... | collective-permute-start | bytes 589832 | tf_op jit(solution)/shard_map/while/body/eval_jaxpr/ppermute | solution.py:13
  810.3 41.3 %collective-permute-start.3 = (bf16[2,6,64,128]{2,3,1,0:T(8,128)(2,1)S(1)}, bf16[2,6,64,128]{2,3,1,0:T(8,128)(2,1)}, u32[]{:S(2)}, u32[]{:S(2)}) collective-permute-start(bf16[2,6,64,128]{2,3,1,0:T(8,128)(2,1)S(1)} %copy.105), channel_id=1, source_target_pairs={{15,0},{0,1},{1,2},{2,3},{3,4},{4,5},{5,6},{6,7},{7,8},{8,9},{9,10... | collective-permute-start | bytes 589832 | tf_op jit(solution)/shard_map/while/body/eval_jaxpr/ppermute | solution.py:13
  858.8 42.6 %collective-permute-start.4 = (f32[2,6,64,4,32]{2,4,3,1,0:T(8,128)}, f32[2,6,64,4,32]{2,4,3,1,0:T(8,128)}, u32[]{:S(2)}, u32[]{:S(2)}) collective-permute-start(f32[2,6,64,4,32]{2,4,3,1,0:T(8,128)} %fusion.92), channel_id=1, source_target_pairs={{15,0},{0,1},{1,2},{2,3},{3,4},{4,5},{5,6},{6,7},{7,8},{8,9},{9,10... | collective-permute-start | bytes 1179656 | tf_op jit(solution)/shard_map/while/body/eval_jaxpr/ppermute | solution.py:13
  860.0 41.4 %collective-permute-start.5 = (f32[2,6,64,4,32]{2,4,3,1,0:T(8,128)}, f32[2,6,64,4,32]{2,4,3,1,0:T(8,128)S(1)}, u32[]{:S(2)}, u32[]{:S(2)}) collective-permute-start(f32[2,6,64,4,32]{2,4,3,1,0:T(8,128)} %fusion.93), channel_id=1, source_target_pairs={{15,0},{0,1},{1,2},{2,3},{3,4},{4,5},{5,6},{6,7},{7,8},{8,9},{9,10... | collective-permute-start | bytes 1179656 | tf_op jit(solution)/shard_map/while/body/eval_jaxpr/ppermute | solution.py:13
  860.0 36.7 %collective-permute-start.2 = (bf16[2,6,64,128]{2,3,1,0:T(8,128)(2,1)S(1)}, bf16[2,6,64,128]{2,3,1,0:T(8,128)(2,1)}, u32[]{:S(2)}, u32[]{:S(2)}) collective-permute-start(bf16[2,6,64,128]{2,3,1,0:T(8,128)(2,1)S(1)} %copy.104), channel_id=1, source_target_pairs={{15,0},{0,1},{1,2},{2,3},{3,4},{4,5},{5,6},{6,7},{7,8},{8,9},{9,10... | collective-permute-start | bytes 589832 | tf_op jit(solution)/shard_map/while/body/eval_jaxpr/ppermute | solution.py:13
  860.0 41.3 %collective-permute-start.3 = (bf16[2,6,64,128]{2,3,1,0:T(8,128)(2,1)S(1)}, bf16[2,6,64,128]{2,3,1,0:T(8,128)(2,1)}, u32[]{:S(2)}, u32[]{:S(2)}) collective-permute-start(bf16[2,6,64,128]{2,3,1,0:T(8,128)(2,1)S(1)} %copy.105), channel_id=1, source_target_pairs={{15,0},{0,1},{1,2},{2,3},{3,4},{4,5},{5,6},{6,7},{7,8},{8,9},{9,10... | collective-permute-start | bytes 589832 | tf_op jit(solution)/shard_map/while/body/eval_jaxpr/ppermute | solution.py:13
  908.5 43.0 %collective-permute-start.4 = (f32[2,6,64,4,32]{2,4,3,1,0:T(8,128)}, f32[2,6,64,4,32]{2,4,3,1,0:T(8,128)}, u32[]{:S(2)}, u32[]{:S(2)}) collective-permute-start(f32[2,6,64,4,32]{2,4,3,1,0:T(8,128)} %fusion.92), channel_id=1, source_target_pairs={{15,0},{0,1},{1,2},{2,3},{3,4},{4,5},{5,6},{6,7},{7,8},{8,9},{9,10... | collective-permute-start | bytes 1179656 | tf_op jit(solution)/shard_map/while/body/eval_jaxpr/ppermute | solution.py:13
  909.7 41.8 %collective-permute-start.5 = (f32[2,6,64,4,32]{2,4,3,1,0:T(8,128)}, f32[2,6,64,4,32]{2,4,3,1,0:T(8,128)S(1)}, u32[]{:S(2)}, u32[]{:S(2)}) collective-permute-start(f32[2,6,64,4,32]{2,4,3,1,0:T(8,128)} %fusion.93), channel_id=1, source_target_pairs={{15,0},{0,1},{1,2},{2,3},{3,4},{4,5},{5,6},{6,7},{7,8},{8,9},{9,10... | collective-permute-start | bytes 1179656 | tf_op jit(solution)/shard_map/while/body/eval_jaxpr/ppermute | solution.py:13
  909.7 37.6 %collective-permute-start.2 = (bf16[2,6,64,128]{2,3,1,0:T(8,128)(2,1)S(1)}, bf16[2,6,64,128]{2,3,1,0:T(8,128)(2,1)}, u32[]{:S(2)}, u32[]{:S(2)}) collective-permute-start(bf16[2,6,64,128]{2,3,1,0:T(8,128)(2,1)S(1)} %copy.104), channel_id=1, source_target_pairs={{15,0},{0,1},{1,2},{2,3},{3,4},{4,5},{5,6},{6,7},{7,8},{8,9},{9,10... | collective-permute-start | bytes 589832 | tf_op jit(solution)/shard_map/while/body/eval_jaxpr/ppermute | solution.py:13
  909.7 41.8 %collective-permute-start.3 = (bf16[2,6,64,128]{2,3,1,0:T(8,128)(2,1)S(1)}, bf16[2,6,64,128]{2,3,1,0:T(8,128)(2,1)}, u32[]{:S(2)}, u32[]{:S(2)}) collective-permute-start(bf16[2,6,64,128]{2,3,1,0:T(8,128)(2,1)S(1)} %copy.105), channel_id=1, source_target_pairs={{15,0},{0,1},{1,2},{2,3},{3,4},{4,5},{5,6},{6,7},{7,8},{8,9},{9,10... | collective-permute-start | bytes 589832 | tf_op jit(solution)/shard_map/while/body/eval_jaxpr/ppermute | solution.py:13
  958.6 44.1 %collective-permute-start.4 = (f32[2,6,64,4,32]{2,4,3,1,0:T(8,128)}, f32[2,6,64,4,32]{2,4,3,1,0:T(8,128)}, u32[]{:S(2)}, u32[]{:S(2)}) collective-permute-start(f32[2,6,64,4,32]{2,4,3,1,0:T(8,128)} %fusion.92), channel_id=1, source_target_pairs={{15,0},{0,1},{1,2},{2,3},{3,4},{4,5},{5,6},{6,7},{7,8},{8,9},{9,10... | collective-permute-start | bytes 1179656 | tf_op jit(solution)/shard_map/while/body/eval_jaxpr/ppermute | solution.py:13
  959.9 42.9 %collective-permute-start.5 = (f32[2,6,64,4,32]{2,4,3,1,0:T(8,128)}, f32[2,6,64,4,32]{2,4,3,1,0:T(8,128)S(1)}, u32[]{:S(2)}, u32[]{:S(2)}) collective-permute-start(f32[2,6,64,4,32]{2,4,3,1,0:T(8,128)} %fusion.93), channel_id=1, source_target_pairs={{15,0},{0,1},{1,2},{2,3},{3,4},{4,5},{5,6},{6,7},{7,8},{8,9},{9,10... | collective-permute-start | bytes 1179656 | tf_op jit(solution)/shard_map/while/body/eval_jaxpr/ppermute | solution.py:13
  959.9 38.6 %collective-permute-start.2 = (bf16[2,6,64,128]{2,3,1,0:T(8,128)(2,1)S(1)}, bf16[2,6,64,128]{2,3,1,0:T(8,128)(2,1)}, u32[]{:S(2)}, u32[]{:S(2)}) collective-permute-start(bf16[2,6,64,128]{2,3,1,0:T(8,128)(2,1)S(1)} %copy.104), channel_id=1, source_target_pairs={{15,0},{0,1},{1,2},{2,3},{3,4},{4,5},{5,6},{6,7},{7,8},{8,9},{9,10... | collective-permute-start | bytes 589832 | tf_op jit(solution)/shard_map/while/body/eval_jaxpr/ppermute | solution.py:13
  959.9 42.9 %collective-permute-start.3 = (bf16[2,6,64,128]{2,3,1,0:T(8,128)(2,1)S(1)}, bf16[2,6,64,128]{2,3,1,0:T(8,128)(2,1)}, u32[]{:S(2)}, u32[]{:S(2)}) collective-permute-start(bf16[2,6,64,128]{2,3,1,0:T(8,128)(2,1)S(1)} %copy.105), channel_id=1, source_target_pairs={{15,0},{0,1},{1,2},{2,3},{3,4},{4,5},{5,6},{6,7},{7,8},{8,9},{9,10... | collective-permute-start | bytes 589832 | tf_op jit(solution)/shard_map/while/body/eval_jaxpr/ppermute | solution.py:13
  1009.9 45.2 %collective-permute-start.4 = (f32[2,6,64,4,32]{2,4,3,1,0:T(8,128)}, f32[2,6,64,4,32]{2,4,3,1,0:T(8,128)}, u32[]{:S(2)}, u32[]{:S(2)}) collective-permute-start(f32[2,6,64,4,32]{2,4,3,1,0:T(8,128)} %fusion.92), channel_id=1, source_target_pairs={{15,0},{0,1},{1,2},{2,3},{3,4},{4,5},{5,6},{6,7},{7,8},{8,9},{9,10... | collective-permute-start | bytes 1179656 | tf_op jit(solution)/shard_map/while/body/eval_jaxpr/ppermute | solution.py:13
  1011.1 43.9 %collective-permute-start.5 = (f32[2,6,64,4,32]{2,4,3,1,0:T(8,128)}, f32[2,6,64,4,32]{2,4,3,1,0:T(8,128)S(1)}, u32[]{:S(2)}, u32[]{:S(2)}) collective-permute-start(f32[2,6,64,4,32]{2,4,3,1,0:T(8,128)} %fusion.93), channel_id=1, source_target_pairs={{15,0},{0,1},{1,2},{2,3},{3,4},{4,5},{5,6},{6,7},{7,8},{8,9},{9,10... | collective-permute-start | bytes 1179656 | tf_op jit(solution)/shard_map/while/body/eval_jaxpr/ppermute | solution.py:13
  1011.1 39.7 %collective-permute-start.2 = (bf16[2,6,64,128]{2,3,1,0:T(8,128)(2,1)S(1)}, bf16[2,6,64,128]{2,3,1,0:T(8,128)(2,1)}, u32[]{:S(2)}, u32[]{:S(2)}) collective-permute-start(bf16[2,6,64,128]{2,3,1,0:T(8,128)(2,1)S(1)} %copy.104), channel_id=1, source_target_pairs={{15,0},{0,1},{1,2},{2,3},{3,4},{4,5},{5,6},{6,7},{7,8},{8,9},{9,10... | collective-permute-start | bytes 589832 | tf_op jit(solution)/shard_map/while/body/eval_jaxpr/ppermute | solution.py:13
  1011.1 43.9 %collective-permute-start.3 = (bf16[2,6,64,128]{2,3,1,0:T(8,128)(2,1)S(1)}, bf16[2,6,64,128]{2,3,1,0:T(8,128)(2,1)}, u32[]{:S(2)}, u32[]{:S(2)}) collective-permute-start(bf16[2,6,64,128]{2,3,1,0:T(8,128)(2,1)S(1)} %copy.105), channel_id=1, source_target_pairs={{15,0},{0,1},{1,2},{2,3},{3,4},{4,5},{5,6},{6,7},{7,8},{8,9},{9,10... | collective-permute-start | bytes 589832 | tf_op jit(solution)/shard_map/while/body/eval_jaxpr/ppermute | solution.py:13
  1075.8 24.1 %collective-permute-start.7 = (f32[2,6,64,4,32]{2,4,3,1,0:T(8,128)S(1)}, f32[2,6,64,4,32]{2,4,3,1,0:T(8,128)S(1)}, u32[]{:S(2)}, u32[]{:S(2)}) collective-permute-start(f32[2,6,64,4,32]{2,4,3,1,0:T(8,128)S(1)} %fusion.19), channel_id=1, source_target_pairs={{15,0},{0,1},{1,2},{2,3},{3,4},{4,5},{5,6},{6,7},{7,8},{8,9},{9,10... | collective-permute-start | bytes 1179656 | tf_op jit(solution)/shard_map/ppermute | solution.py:13
  (37 other events, 757.0 us)
Sparse Core Ops, SparseCore 0:
  1072.7 89.6 reduce-scatter.3
where the time goes:
time: 1180 us; the launch traced here: 1170 us
  waiting for transfers between devices  864 us (73%)
  matrix products  145 us (12%)
  local copies, waits for them, and re-layouts  111 us (9%)
  other arithmetic  27.1 us (2%)
  between operations  14.3 us (1%)
    ppermute x92, waiting for transfers between devices, from_behind(): return lax.ppermute(block, axis, route)  803 us
    unnamed x2, waiting for transfers between devices  61.5 us
    dot_general x64, matrix products, pair_products(): jnp.einsum('crjhd,crkhd->crhjk', split_heads(left), split_heads(right), p...  48.4 us
    dot_general x16, matrix products, query_update(): jnp.einsum('crhjk,crkhd->crjhd', dscores_half, split_heads(key_tile), pre...  39.5 us
    dynamic_update_slice x16, local copies, waits for them, and re-layouts, query_update(): lax.dynamic_update_slice_in_dim(bias_part, jnp.sum(dscores, axis=1), key_...  39.1 us
    dot_general x16, matrix products, carry_update(): jnp.einsum('crhjk,crjhd->crkhd', dscores_half, split_heads(query), prefer...  38.1 us
    while x75, local copies, waits for them, and re-layouts  30.8 us
  transfers between devices with their start and end apart: 93, of which 63 were waited for; matrix products, arithmetic and copies ran while one was open for 12% of the time, Pallas kernels for 0%

commit v1 on v0

v1 whole, which is shorter than its diff:
```python
import functools
import jax, jax.numpy as jnp
from jax import lax
from jax.sharding import PartitionSpec as P
from jax.experimental import pallas as pl
from jax.experimental.pallas import tpu as pltpu
HD=32; SEQ=1024; NP=3
LOG2E=1.4426950408889634
SCALE=HD**-0.5
B=256
R=16

def nt(a,b): return lax.dot_general(a,b,(((1,),(1,)),((),())),preferred_element_type=jnp.float32)
def nn(a,b): return lax.dot_general(a,b,(((1,),(0,)),((),())),preferred_element_type=jnp.float32)

def prep(p, t_ref, tt, tq, td, kr):
    lane = lax.broadcasted_iota(jnp.int32,(SEQ,128),1)
    x = t_ref[p]
    tt[p] = x.T
    zero = jnp.zeros_like(x)
    tq[p] = jnp.where(lane<HD, x, zero)
    td[p] = jnp.where((lane>=HD)&(lane<2*HD), x, zero)
    y = pltpu.roll(x.astype(jnp.float32), 64, 1).astype(jnp.bfloat16)
    kr[p] = jnp.where(lane<HD, y, zero)

def kernel(len_ref, t_ref, bias_ref, g_ref, db_ref, tt, tq, td, kr, s_ref, dp_ref, b2_ref, ph, dsh, dkt, dvt, dq):
    n = len_ref[0]
    for p in range(NP):
        prep(p, t_ref, tt, tq, td, kr)
    dkt[...] = jnp.zeros_like(dkt); dvt[...] = jnp.zeros_like(dvt)
    def jblock(jb, _):
        j0 = pl.multiple_of(jb*B, B)
        rows = pl.ds(j0, B)
        for p in range(NP):
            rt = jnp.concatenate([tt[p,64:128],tt[p,0:64]],axis=0)
            s_ref[p%2] = nn(tq[p,rows,:], rt)
            dp_ref[p%2] = nn(td[p,rows,:], rt)
            for c in range(B//R):
                r = pl.ds(c*R,R)
                jr = pl.ds(j0+c*R,R)
                if p==0:
                    col = lax.broadcasted_iota(jnp.int32,(R,SEQ),1)
                    b2 = jnp.where(col<n, bias_ref[jr,:].astype(jnp.float32)*LOG2E, -1e30)
                    b2_ref[r,:] = b2
                else:
                    b2 = b2_ref[r,:]
                s = s_ref[p%2,r,:]*(SCALE*LOG2E)+b2
                m = jnp.max(s,axis=1,keepdims=True)
                e = jnp.exp2(s-m)
                dp = dp_ref[p%2,r,:]
                l = jnp.sum(e,axis=1,keepdims=True)
                w = jnp.sum(e*dp,axis=1,keepdims=True)
                rl = 1.0/l
                pr = e*rl
                ds = pr*(dp-w*rl)
                ph[p%2,r,:] = pr.astype(jnp.bfloat16)
                dsh[p%2,r,:] = ds.astype(jnp.bfloat16)
                if p==0: db_ref[jr,:] = ds
                else: db_ref[jr,:] += ds
            dsv = dsh[p%2]
            dq[p,rows,:] = nn(dsv, kr[p])
            dkt[p] += nn(tt[p,0:32,rows], dsv)
            dvt[p] += nn(tt[p,32:64,rows], ph[p%2])
        return 0
    lax.fori_loop(0, SEQ//B, jblock, 0)
    for p in range(NP):
        z = jnp.zeros((HD,SEQ),jnp.float32)
        acc = jnp.concatenate([z,dkt[p]*SCALE,dvt[p],z],axis=0)
        g_ref[p] = (acc.T + dq[p]*SCALE).astype(jnp.bfloat16)

def attn(n, t, bias):
    V=pltpu.VMEM; bf=jnp.bfloat16; f=jnp.float32
    return pl.pallas_call(kernel,
      out_shape=(jax.ShapeDtypeStruct((NP,SEQ,128),bf), jax.ShapeDtypeStruct((SEQ,SEQ),f)),
      in_specs=[pl.BlockSpec(memory_space=pltpu.SMEM),pl.BlockSpec(memory_space=V),pl.BlockSpec(memory_space=V)],
      out_specs=(pl.BlockSpec(memory_space=V),pl.BlockSpec(memory_space=V)),
      scratch_shapes=[V((NP,128,SEQ),bf),V((NP,SEQ,128),bf),V((NP,SEQ,128),bf),V((NP,SEQ,128),bf),
        V((2,B,SEQ),f),V((2,B,SEQ),f),V((B,SEQ),f),V((2,B,SEQ),bf),V((2,B,SEQ),bf),
        V((NP,HD,SEQ),f),V((NP,HD,SEQ),f),V((NP,SEQ,128),f)],
      compiler_params=pltpu.CompilerParams(vmem_limit_bytes=60*2**20),
    )(n,t,bias)


def per_device(query, key, value, grad_out, pair_bias, crop_lengths):
    me_col = lax.axis_index("col")
    me_row = lax.axis_index("row")
    def heads(x):
        return x.reshape(2, 2, 3, 64, 4, HD)
    t = jnp.concatenate([heads(query), heads(grad_out), heads(key), heads(value)], axis=-1)
    t = t.transpose(0, 4, 1, 2, 3, 5).reshape(16, 3, 64, 128)
    t = lax.all_to_all(t, "col", 0, 0, tiled=False)
    t = t.transpose(1, 0, 2, 3).reshape(3, SEQ, 128)
    part = lax.dynamic_slice_in_dim(pair_bias, me_row * 4, 4, 2).reshape(8, 1, 4, SEQ)
    part = jnp.broadcast_to(part, (8, 2, 4, SEQ)).reshape(16, 4, SEQ)
    part = lax.all_to_all(part, "col", 0, 0, tiled=False)
    bias = lax.all_gather(part, "row", axis=1, tiled=True).reshape(SEQ, SEQ)
    n = lax.dynamic_slice(crop_lengths, (me_col // 8,), (1,))
    g, db = attn(n, t, bias)
    g = g.reshape(3, 16, 64, 128).transpose(1, 0, 2, 3)
    g = lax.all_to_all(g, "col", 0, 0, tiled=False)
    g = g.reshape(2, 4, 2, 3, 64, 4, HD).transpose(5, 0, 2, 3, 4, 1, 6).reshape(4, 2, 6, 64, 128).astype(jnp.float32)
    db = lax.psum_scatter(db, "row", scatter_dimension=1, tiled=True).reshape(16, 64, 64)
    db = lax.all_to_all(db, "col", 0, 0, tiled=False)
    db = db.reshape(2, 4, 2, 64, 64).sum(2)
    return g[0], g[1], g[2], db


def solution(mesh):
    spec = P(None, "row", "col", None)
    return jax.shard_map(
        per_device,
        mesh=mesh,
        in_specs=(spec, spec, spec, spec, P(None, None, "col", None), P()),
        out_specs=(spec, spec, spec, P(None, None, "col", "row")),
        check_vma=False,
    )
```

time: 1180 us -> 196 us (0.17)
  waiting for transfers between devices: 864 us -> 62.7 us
  matrix products: 145 us -> 0 us
  local copies, waits for them, and re-layouts: 111 us -> 28.7 us
  blocking collectives: 0 us -> 51.5 us
  other arithmetic: 27.1 us -> 4.97 us
  Pallas kernels: 0 us -> 17.2 us
    ppermute x92 -> x0, waiting for transfers between devices: 803 us -> none  [from_behind(): return lax.ppermute(block, axis, route)]
    dot_general x112 -> x0, matrix products: 145 us -> none  [the longest x64 48.4 us: pair_products(): jnp.einsum('crjhd,crkhd->crhjk', split_heads(left), split_heads(right), p...]
    all_to_all x0 -> x2, blocking collectives: none -> 51.5 us  [the longest x1 31 us: per_device(): g = lax.all_to_all(g, 'col', 0, 0, tiled=False)]
    dynamic_update_slice x16 -> x0, local copies, waits for them, and re-layouts: 39.1 us -> none  [query_update(): lax.dynamic_update_slice_in_dim(bias_part, jnp.sum(dscores, axis=1), key_...]
    while x75 -> x0, local copies, waits for them, and re-layouts: 30.8 us -> none
    unnamed x2 -> x3, waiting for transfers between devices: 61.5 us -> 35.6 us
    all_to_all x0 -> x2, waiting for transfers between devices: none -> 24.2 us  [the longest x1 18.8 us: per_device(): t = lax.all_to_all(t, 'col', 0, 0, tiled=False)]
    pallas_call x0 -> x1, Pallas kernels: none -> 17.2 us  [attn(): pl.pallas_call(kernel, out_shape=(jax.ShapeDtypeStruct((NP, SEQ, 128), bf...]
  transfers between devices with their start and end apart: 93 -> 4, of which waited for: 63 -> 4; matrix products, arithmetic and copies ran while one was open for 12% -> 8% of each run, Pallas kernels for 0% -> 0%
where the time goes in v1:
time: 196 us; the launch traced here: 192 us
  waiting for transfers between devices  62.7 us (32%)
  blocking collectives  51.5 us (26%)
  local copies, waits for them, and re-layouts  28.7 us (15%)
  Pallas kernels  17.2 us (9%)
  between operations  14.2 us (7%)
  starting transfers between devices  12.8 us (7%)
  other arithmetic  4.97 us (3%)
    unnamed x3, waiting for transfers between devices  35.6 us
    all_to_all x1, blocking collectives, per_device(): g = lax.all_to_all(g, 'col', 0, 0, tiled=False)  31 us
    all_to_all x1, blocking collectives, per_device(): part = lax.all_to_all(part, 'col', 0, 0, tiled=False)  20.5 us
    unnamed x17, local copies, waits for them, and re-layouts  19.1 us
    all_to_all x1, waiting for transfers between devices, per_device(): t = lax.all_to_all(t, 'col', 0, 0, tiled=False)  18.8 us
    pallas_call x1, Pallas kernels, attn(): pl.pallas_call(kernel, out_shape=(jax.ShapeDtypeStruct((NP, SEQ, 128), bf...  17.2 us
    all_to_all x1, starting transfers between devices, per_device(): db = lax.all_to_all(db, 'col', 0, 0, tiled=False)  9.09 us
    all_to_all x1, waiting for transfers between devices, per_device(): db = lax.all_to_all(db, 'col', 0, 0, tiled=False)  5.42 us
  transfers between devices with their start and end apart: 4, of which 4 were waited for; matrix products, arithmetic and copies ran while one was open for 8% of the time, Pallas kernels for 0%

profile of v1, /device:TPU:1, one launch (start us, length us, event | category | flops | bytes accessed | tf_op | source)
XLA Modules:
  0.0 192.1 jit_solution(13869520811214493350)
XLA Ops:
  7.2 0.0 copy-start
  7.2 0.0 all-gather.2.cloned.1.call-start
  7.2 1.2 copy-done
  8.5 20.5 %all_to_all.20 = bf16[16,4,1024]{2,1,0:T(4,128)(2,1)S(1)} all-to-all(bf16[16,4,1024]{2,1,0:T(4,128)(2,1)S(1)} %bitcast.43), channel_id=1, replica_groups=mesh['row'=16,'col'=16] {'col'}, dimensions={0} | all-to-all | bytes 262144 | tf_op jit(solution)/shard_map/all_to_all | solution.py:95
  29.0 0.7 copy.73
  29.7 0.0 all-gather.2.cloned.1.call-update
  29.7 1.2 copy.67
  30.9 1.2 copy.68
  32.0 1.9 copy.69
  33.9 1.8 copy.70
  35.7 0.0 copy-start.2
  35.7 1.6 maximum_bitcast_fusion
  37.3 1.4 copy.71
  38.7 3.6 %all-to-all-start = ((bf16[16,3,64,128]{3,2,1,0:T(8,128)(2,1)}), bf16[16,3,64,128]{3,2,1,0:T(8,128)(2,1)S(1)}, u32[]{:S(2)}, u32[]{:S(2)}) async-start(bf16[16,3,64,128]{3,2,1,0:T(8,128)(2,1)} %bitcast.7), calls=%async_computation | async-start | bytes 1572864 | tf_op jit(solution)/shard_map/all_to_all | solution.py:91
  42.3 0.0 reduce-scatter.4.cloned.1.call-start
  42.4 0.0 copy-done.2
  42.4 0.6 dynamic_slice.6.len_ref
  43.0 18.8 %all-to-all-done = bf16[16,3,64,128]{3,2,1,0:T(8,128)(2,1)S(1)} async-done(((bf16[16,3,64,128]{3,2,1,0:T(8,128)(2,1)}), bf16[16,3,64,128]{3,2,1,0:T(8,128)(2,1)S(1)}, u32[]{:S(2)}, u32[]{:S(2)}) %all-to-all-start) | async-done | bytes 786464 | tf_op jit(solution)/shard_map/all_to_all | solution.py:91
  61.8 1.0 copy.72
  62.7 2.9 %all-gather.2.cloned.1.call-done = bf16[16,64,1024]{2,0,1:T(8,128)(2,1)} async-done(((bf16[16,4,1024]{2,0,1:T(8,128)(2,1)}), bf16[16,64,1024]{2,0,1:T(8,128)(2,1)}) %all-gather.2.cloned.1.call-update) | async-done | bytes 2097168 | tf_op jit(solution)/shard_map/all_gather | solution.py:96
  65.6 4.1 %copy.74 = bf16[16,64,1024]{2,1,0:T(8,128)(2,1)} copy(bf16[16,64,1024]{2,0,1:T(8,128)(2,1)} %all-gather.2.cloned.1.call-done) | data formatting | bytes 4194304 | tf_op jit(solution)/shard_map/all_gather | solution.py:96
  69.6 17.2 %shard_map.93 = (bf16[3,1024,128]{2,1,0:T(8,128)(2,1)}, f32[1024,1024]{1,0:T(8,128)}) custom-call(s32[1]{0:T(128)} %dynamic_slice.6.len_ref, bf16[3,1024,128]{2,1,0:T(8,128)(2,1)} %bitcast.36, bf16[1024,1024]{1,0:T(8,128)(2,1)} %bitcast.29), custom_call_target="tpu_custom_call" | custom-call | tf_op jit(solution)/shard_map/pallas_call | solution.py:73
  86.9 5.4 %copy.83 = f32[1024,1024]{0,1:T(8,128)} copy(f32[1024,1024]{1,0:T(8,128)} %get-tuple-element.7) | data formatting | bytes 8388608
  92.2 0.0 copy-start.1
  92.3 0.0 reduce-scatter.4.cloned.1.call-update
  92.3 1.1 copy-done.1
  93.4 0.1 copy.86
  93.4 31.0 %all_to_all.21 = bf16[16,3,64,128]{3,2,1,0:T(8,128)(2,1)S(1)} all-to-all(bf16[16,3,64,128]{3,2,1,0:T(8,128)(2,1)S(1)} %bitcast.32), channel_id=1, replica_groups=mesh['row'=16,'col'=16] {'col'}, dimensions={0} | all-to-all | bytes 1572864 | tf_op jit(solution)/shard_map/all_to_all | solution.py:100
  124.5 0.9 copy.76
  125.3 35.6 %reduce-scatter.4.cloned.1.call-done = f32[64,1024]{1,0:T(8,128)} async-done(((f32[1024,1024]{1,0:T(8,128)}), f32[64,1024]{1,0:T(8,128)}) %reduce-scatter.4.cloned.1.call-update) | async-done | bytes 262160
  160.9 1.1 copy.84
  162.1 1.0 reshape.68
  163.1 9.1 %all-to-all-start.3 = ((f32[16,1,4096]{2,1,0:T(1,128)}), f32[16,1,4096]{2,1,0:T(1,128)}, u32[]{:S(2)}, u32[]{:S(2)}) async-start(f32[16,1,4096]{2,1,0:T(1,128)} %reshape.68), calls=%async_computation.3 | async-start | bytes 524288 | tf_op jit(solution)/shard_map/all_to_all | solution.py:103
  172.2 0.4 convert_bitcast_fusion
  172.6 0.2 fusion
  172.9 0.1 copy.77
  173.0 1.0 copy.80
  174.0 0.1 copy.78
  174.0 1.0 copy.81
  175.0 0.1 copy.79
  175.1 1.0 copy.82
  176.1 5.4 %all-to-all-done.3 = f32[16,1,4096]{2,1,0:T(1,128)} async-done(((f32[16,1,4096]{2,1,0:T(1,128)}), f32[16,1,4096]{2,1,0:T(1,128)}, u32[]{:S(2)}, u32[]{:S(2)}) %all-to-all-start.3) | async-done | bytes 262176 | tf_op jit(solution)/shard_map/all_to_all | solution.py:103
  181.5 0.5 broadcast.1
  182.0 2.2 %reduce = f32[16,4096]{1,0:T(8,128)S(1)} reduce(f32[16,1,4096]{2,1,0:T(1,128)} %all-to-all-done.3, f32[]{:T(128)} %broadcast.1), dimensions={1}, to_apply=%all_to_all.15.reduce_sub_computation | reduce | bytes 524292 | tf_op jit(solution)/shard_map/all_to_all | solution.py:103
  184.3 0.2 reshape.69
  184.5 0.7 bitcast_reduce_fusion
  (2 shorter events, 0.1 us)
Async XLA Ops:
  7.2 1.2 copy-start
  7.2 58.4 %all-gather.2.cloned.1.call-start = ((), (), s32[]{:S(2)}) async-start(), calls=%async_computation.5 | async-start | bytes 2228224 | tf_op jit(solution)/shard_map/all_gather | solution.py:96
  35.7 6.7 %copy-start.2 = (s32[2]{0:T(128)S(1)}, s32[2]{0:T(128)}, u32[]{:S(2)}) copy-start(s32[2]{0:T(128)} %param.11) | copy-start | bytes 28
  38.7 23.1 %all-to-all-start = ((bf16[16,3,64,128]{3,2,1,0:T(8,128)(2,1)}), bf16[16,3,64,128]{3,2,1,0:T(8,128)(2,1)S(1)}, u32[]{:S(2)}, u32[]{:S(2)}) async-start(bf16[16,3,64,128]{3,2,1,0:T(8,128)(2,1)} %bitcast.7), calls=%async_computation | async-start | bytes 1572864 | tf_op jit(solution)/shard_map/all_to_all | solution.py:91
  42.3 118.6 %reduce-scatter.4.cloned.1.call-start = ((), (), s32[]{:S(2)}) async-start(), calls=%async_computation.6 | async-start | bytes 4456448
  92.2 1.1 copy-start.1
  163.1 18.4 %all-to-all-start.3 = ((f32[16,1,4096]{2,1,0:T(1,128)}), f32[16,1,4096]{2,1,0:T(1,128)}, u32[]{:S(2)}, u32[]{:S(2)}) async-start(f32[16,1,4096]{2,1,0:T(1,128)} %reshape.68), calls=%async_computation.3 | async-start | bytes 524288 | tf_op jit(solution)/shard_map/all_to_all | solution.py:103
Sparse Core Ops, SparseCore 0:
  29.8 35.7 all-gather.1
  92.4 68.4 reduce-scatter.3

commit v2 on v1

v2 whole, which is shorter than its diff:
```python
import functools

import jax
import jax.numpy as jnp
from jax import lax
from jax.experimental import pallas as pl
from jax.experimental.pallas import tpu as pltpu
from jax.sharding import PartitionSpec as P

H = 4
HD = 32
SEQ = 1024
NCOL = 16
BLK = SEQ // NCOL
NP = 3
NCHIP = 8
B = 256
NJ = SEQ // B
R = 16
HALF = B // 2
LOG2E = 1.4426950408889634
SCALE = HD**-0.5
F32 = jnp.float32
BF16 = jnp.bfloat16


def nn(a, b):
    return lax.dot_general(a, b, (((1,), (0,)), ((), ())), preferred_element_type=F32)


def wait_for(ref, sem):
    pltpu.make_async_copy(ref, ref, sem).wait()


def send(src, dst, send_sem, recv_sem, where):
    pltpu.make_async_remote_copy(
        src_ref=src,
        dst_ref=dst,
        send_sem=send_sem,
        recv_sem=recv_sem,
        device_id=where,
        device_id_type=pl.DeviceIdType.MESH,
    ).start()


def kernel(
    len_ref, q_ref, k_ref, v_ref, g_ref, bias_ref,
    dq_out, dk_out, dv_out, db_out,
    tsend, tall, bias_full, b2, tt, tq, td, kr, s_ref, dp_ref, ph, dsh, dkt, dvt, dq,
    gsend, gin, db, sib, rsend, red, fsend, fin, last, lastin,
    t_ss, t_rs, b1_ss, b1_rs, b1_ls, b2_ss, b2_rs, b3_ss, b3_rs, g_ss, g_rs,
    a_ss, a_rs, r_ss, r_rs, f_ss, f_rs, l_ss, l_rs,
):
    row = lax.axis_index("row")
    me = lax.axis_index("col")
    chip = row // 2
    core = row % 2
    sibling = {"row": row + 1 - 2 * core}

    def peer(o):
        return lax.rem(me + o, NCOL)

    def row_peer(o):
        return lax.rem(chip + o, NCHIP)

    barrier = pltpu.get_barrier_semaphore()
    for o in range(1, NCOL):
        pl.semaphore_signal(barrier, inc=1, device_id={"col": peer(o)}, device_id_type=pl.DeviceIdType.MESH)
    for o in range(1, NCHIP):
        pl.semaphore_signal(barrier, inc=1, device_id={"row": 2 * row_peer(o) + core}, device_id_type=pl.DeviceIdType.MESH)
    pl.semaphore_signal(barrier, inc=1, device_id=sibling, device_id_type=pl.DeviceIdType.MESH)

    block_of = lax.broadcasted_iota(jnp.int32, (BLK, 128), 1) // HD

    def pack(p):
        for c in range(2):
            for half in range(2):
                i = half * 3 + p
                arrays = [x[c, i].astype(F32) for x in (q_ref, g_ref, k_ref, v_ref)]
                for h in range(H):
                    out = None
                    for a in range(4):
                        d = (a - h) % 4
                        x = arrays[a] if d == 0 else pltpu.roll(arrays[a], d * HD, 1)
                        out = x if out is None else jnp.where(block_of == a, x, out)
                    tsend[p, c * 8 + h * 2 + half] = out.astype(BF16)
        tall[p, pl.ds(pl.multiple_of(me * BLK, BLK), BLK), :] = tsend[p, me]

    def send_pack(p):
        for o in range(1, NCOL):
            to = peer(o)
            send(
                tsend.at[p, to],
                tall.at[p, pl.ds(pl.multiple_of(me * BLK, BLK), BLK)],
                t_ss.at[p],
                t_rs.at[p],
                {"col": to},
            )

    pack(0)
    pl.semaphore_wait(barrier, NCOL - 1 + NCHIP - 1 + 1)

    my_rows = pl.ds(pl.multiple_of(core * 32 + (chip // 4) * 16, 16), 16)
    my_lanes = pl.ds(pl.multiple_of((chip % 4) * 256, 256), 256)
    for o in range(1, NCOL):
        to = peer(o)
        send(
            bias_ref.at[to // 8, (to // 2) % 4, my_rows, my_lanes],
            bias_full.at[me, my_rows, my_lanes],
            b1_ss,
            b1_rs,
            {"col": to},
        )
    own = pltpu.make_async_copy(
        bias_ref.at[me // 8, (me // 2) % 4, my_rows, my_lanes],
        bias_full.at[me, my_rows, my_lanes],
        b1_ls,
    )
    own.start()
    send_pack(0)
    pack(1)
    send_pack(1)
    pack(2)
    send_pack(2)
    own.wait()
    wait_for(bias_full.at[pl.ds(0, NCOL - 1), pl.ds(0, 16), pl.ds(0, 256)], b1_rs)
    for jb in range(NJ):
        mine = bias_full.at[pl.ds(jb * 4, 4), my_rows, my_lanes]
        for o in range(1, NCHIP):
            send(mine, mine, b2_ss.at[jb], b2_rs.at[jb], {"row": 2 * row_peer(o) + core})

    def bias_to_sibling(jb):
        wait_for(bias_full.at[pl.ds(0, 7), pl.ds(0, 64), pl.ds(0, 256)], b2_rs.at[jb])
        half = bias_full.at[pl.ds(jb * 4, 4), pl.ds(pl.multiple_of(core * 32, 32), 32)]
        send(half, half, b3_ss.at[jb], b3_rs.at[jb], sibling)

    bias_to_sibling(0)
    n = len_ref[me // 8]
    dkt[...] = jnp.zeros_like(dkt)
    dvt[...] = jnp.zeros_like(dvt)

    def prep(p):
        wait_for(tall.at[p, pl.ds(0, BLK * (NCOL - 1))], t_rs.at[p])
        lane = lax.broadcasted_iota(jnp.int32, (SEQ, 128), 1)
        x = tall[p]
        xt = x.T
        tt[pl.ds(0, 64), :] = xt[64:128]
        tt[pl.ds(64, 64), :] = xt[0:64]
        zero = jnp.zeros_like(x)
        tq[...] = jnp.where(lane < HD, x, zero)
        td[...] = jnp.where((lane >= HD) & (lane < 2 * HD), x, zero)
        y = pltpu.roll(x.astype(F32), 64, 1).astype(BF16)
        kr[...] = jnp.where(lane < HD, y, zero)

    def mask_bias(jb):
        col = lax.broadcasted_iota(jnp.int32, (R, SEQ), 1)
        for c in range(B // R):
            x = bias_full[jb * 4 + c // 4, pl.ds((c % 4) * R, R), :].astype(F32)
            b2[pl.ds(pl.multiple_of(jb * B + c * R, R), R), :] = jnp.where(col < n, x * LOG2E, -1e30)

    def tile(p, jb, first):
        j0 = pl.multiple_of(jb * B, B)
        rows = pl.ds(j0, B)
        rt = tt[...]
        s_ref[...] = nn(tq[rows, :], rt)
        dp_ref[...] = nn(td[rows, :], rt)
        for c in range(B // R):
            r = pl.ds(c * R, R)
            jr = pl.ds(pl.multiple_of(j0 + c * R, R), R)
            s = s_ref[r, :] * (SCALE * LOG2E) + b2[jr, :]
            m = jnp.max(s, axis=1, keepdims=True)
            e = jnp.exp2(s - m)
            dp = dp_ref[r, :]
            rl = 1.0 / jnp.sum(e, axis=1, keepdims=True)
            w = jnp.sum(e * dp, axis=1, keepdims=True)
            pr = e * rl
            ds = pr * (dp - w * rl)
            ph[r, :] = pr.astype(BF16)
            dsh[r, :] = ds.astype(BF16)
            db[jr, :] += ds
        dsv = dsh[...]
        dq[rows, :] = nn(dsv, kr[...])
        dkt[...] += nn(tt[pl.ds(64, 32), rows], dsv)
        dvt[...] += nn(tt[pl.ds(96, 32), rows], ph[...])

    def finish(p):
        z = jnp.zeros((HD, SEQ), F32)
        acc = jnp.concatenate([z, dkt[...] * SCALE, dvt[...], z], axis=0)
        gsend[p] = (acc.T + dq[...] * SCALE).astype(BF16)
        dkt[...] = jnp.zeros_like(dkt)
        dvt[...] = jnp.zeros_like(dvt)
        mine = pl.ds(pl.multiple_of(me * BLK, BLK), BLK)
        gin[p, me] = gsend[p, mine, :]
        for o in range(1, NCOL):
            to = peer(o)
            send(
                gsend.at[p, pl.ds(pl.multiple_of(to * BLK, BLK), BLK)],
                gin.at[p, me],
                g_ss.at[p],
                g_rs.at[p],
                {"col": to},
            )

    def db_to_sibling(jb):
        theirs = db.at[pl.ds(pl.multiple_of(jb * B + (1 - core) * HALF, HALF), HALF)]
        send(theirs, sib.at[jb], a_ss.at[jb], a_rs.at[jb], sibling)

    def db_over_row(jb):
        wait_for(sib.at[jb], a_rs.at[jb])
        for o in range(NCHIP):
            x = (
                db[pl.ds(pl.multiple_of(jb * B + core * HALF, HALF), HALF), pl.ds(o * 128, 128)]
                + sib[jb, :, pl.ds(o * 128, 128)]
            )
            rsend[jb, o] = x.astype(BF16)
        red[jb, chip] = rsend[jb, chip]
        for o in range(1, NCHIP):
            to = row_peer(o)
            send(rsend.at[jb, to], red.at[jb, chip], r_ss.at[jb], r_rs.at[jb], {"row": 2 * to + core})

    def db_to_owner(jb):
        wait_for(red.at[jb, pl.ds(0, NCHIP - 1)], r_rs.at[jb])
        total = red[jb, 0].astype(F32)
        for o in range(1, NCHIP):
            total = total + red[jb, o].astype(F32)
        for e in range(2):
            to = jb * 4 + core * 2 + e
            part = total[e * BLK : (e + 1) * BLK]
            fsend[jb * 2 + e] = part

            @pl.when(to == me)
            def _():
                fin[me] = part

            @pl.when(to != me)
            def _():
                send(fsend.at[jb * 2 + e], fin.at[me], f_ss, f_rs, {"col": to})

    @pl.loop(0, NP * NJ)
    def _(it):
        p = it // NJ
        jb = it % NJ

        @pl.when(jb == 0)
        def _():
            prep(p)

        @pl.when(p == 0)
        def _():
            @pl.when(jb < NJ - 1)
            def _():
                bias_to_sibling(jb + 1)

            wait_for(bias_full.at[pl.ds(0, 4), pl.ds(0, 32)], b3_rs.at[jb])
            mask_bias(jb)

            db[pl.ds(pl.multiple_of(jb * B, B), B), :] = jnp.zeros((B, SEQ), F32)

        tile(p, jb, None)

        @pl.when(p == NP - 1)
        def _():
            db_to_sibling(jb)

        @pl.when(jb == NJ - 1)
        def _():
            finish(p)

        @pl.when((p == NP - 1) & (jb >= 1))
        def _():
            db_over_row(jb - 1)

        @pl.when((p == NP - 1) & (jb >= 2))
        def _():
            db_to_owner(jb - 2)

    db_over_row(NJ - 1)
    db_to_owner(NJ - 2)

    def unpack(p):
        wait_for(gin.at[p, pl.ds(0, NCOL - 1)], g_rs.at[p])
        for c in range(2):
            for half in range(2):
                i = half * 3 + p
                parts = [gin[p, c * 8 + h * 2 + half].astype(F32) for h in range(H)]
                for a, out_ref in enumerate((dq_out, dk_out, dv_out)):
                    out = None
                    for h in range(H):
                        d = (h - a) % 4
                        x = parts[h] if d == 0 else pltpu.roll(parts[h], d * HD, 1)
                        out = x if out is None else jnp.where(block_of == h, x, out)
                    out_ref[c, i] = out

    unpack(0)
    db_to_owner(NJ - 1)
    unpack(1)
    owner = (me // 2) % 2 == core

    def put(value):
        x = jnp.where(core == 0, value, pltpu.roll(value, 64, 1))
        return x[:, 0:64]

    @pl.when(owner)
    def _():
        wait_for(fin.at[pl.ds(0, NCOL - 1)], f_rs)
        for e in range(8):
            x = fin[2 * e] + fin[2 * e + 1]
            last[e] = x
            db_out[e // 4, e % 4] = put(x)
        send(last, lastin, l_ss, l_rs, sibling)

    unpack(2)

    @pl.when(owner)
    def _():
        wait_for(last, l_ss)
        wait_for(fsend.at[pl.ds(0, 7)], f_ss)

    @pl.when(jnp.logical_not(owner))
    def _():
        wait_for(lastin, l_rs)
        for e in range(8):
            db_out[e // 4, e % 4] = put(lastin[e])
        wait_for(fsend, f_ss)

    wait_for(bias_full.at[pl.ds(0, NCOL - 1), pl.ds(0, 16), pl.ds(0, 256)], b1_ss)
    for p in range(NP):
        wait_for(tall.at[p, pl.ds(0, BLK * (NCOL - 1))], t_ss.at[p])
        wait_for(gin.at[p, pl.ds(0, NCOL - 1)], g_ss.at[p])
    for jb in range(NJ):
        wait_for(bias_full.at[pl.ds(0, 7), pl.ds(0, 64), pl.ds(0, 256)], b2_ss.at[jb])
        wait_for(bias_full.at[pl.ds(0, 4), pl.ds(0, 32)], b3_ss.at[jb])
        wait_for(sib.at[jb], a_ss.at[jb])
        wait_for(red.at[jb, pl.ds(0, NCHIP - 1)], r_ss.at[jb])


def per_device(query, key, value, grad_out, pair_bias, crop_lengths):
    V = pltpu.VMEM
    D = pltpu.SemaphoreType.DMA
    grad = jax.ShapeDtypeStruct(query.shape, F32)
    vm = pl.BlockSpec(memory_space=V)
    return pl.pallas_call(
        kernel,
        out_shape=(grad, grad, grad, jax.ShapeDtypeStruct((2, H, BLK, BLK), F32)),
        in_specs=[pl.BlockSpec(memory_space=pltpu.SMEM)] + [vm] * 5,
        out_specs=(vm,) * 4,
        scratch_shapes=[
            V((NP, NCOL, BLK, 128), BF16),
            V((NP, SEQ, 128), BF16),
            V((NCOL, BLK, SEQ), BF16),
            V((SEQ, SEQ), F32),
            V((128, SEQ), BF16),
            V((SEQ, 128), BF16),
            V((SEQ, 128), BF16),
            V((SEQ, 128), BF16),
            V((B, SEQ), F32),
            V((B, SEQ), F32),
            V((B, SEQ), BF16),
            V((B, SEQ), BF16),
            V((HD, SEQ), F32),
            V((HD, SEQ), F32),
            V((SEQ, 128), F32),
            V((NP, SEQ, 128), BF16),
            V((NP, NCOL, BLK, 128), BF16),
            V((SEQ, SEQ), F32),
            V((NJ, HALF, SEQ), F32),
            V((NJ, NCHIP, HALF, 128), BF16),
            V((NJ, NCHIP, HALF, 128), BF16),
            V((8, BLK, 128), F32),
            V((NCOL, BLK, 128), F32),
            V((8, BLK, 128), F32),
            V((8, BLK, 128), F32),
            D((NP,)), D((NP,)), D, D, D, D((NJ,)), D((NJ,)), D((NJ,)), D((NJ,)), D((NP,)), D((NP,)),
            D((NJ,)), D((NJ,)), D((NJ,)), D((NJ,)), D, D, D, D,
        ],
        compiler_params=pltpu.CompilerParams(
            vmem_limit_bytes=60 * 2**20, collective_id=0, has_side_effects=True
        ),
        cost_estimate=pl.CostEstimate(flops=8 * 10**9, bytes_accessed=4 * 10**6, transcendentals=3 * 2**20),
    )(crop_lengths, query, key, value, grad_out, pair_bias)


def solution(mesh):
    spec = P(None, "row", "col", None)
    return jax.shard_map(
        per_device,
        mesh=mesh,
        in_specs=(spec, spec, spec, spec, P(None, None, "col", None), P()),
        out_specs=(spec, spec, spec, P(None, None, "col", "row")),
        check_vma=False,
    )
```

time: 196 us -> 86.3 us (0.44)
  the two profiles are of different devices: /device:TPU:1 before, /device:TPU:17 now
where the time goes in v2:
time: 86.3 us; the launch traced here: 86.1 us
  Pallas kernels  80.7 us (94%)
  local copies, waits for them, and re-layouts  4.75 us (6%)
    pallas_call x1, Pallas kernels, per_device(): pl.pallas_call(kernel, out_shape=(grad, grad, grad, jax.ShapeDtypeStruct(...  80.7 us
    unnamed x10, local copies, waits for them, and re-layouts  4.75 us

profile of v2, /device:TPU:17, one launch (start us, length us, event | category | flops | bytes accessed | tf_op | source)
XLA Modules:
  0.0 86.1 jit_solution(5106175309169594970)
XLA Ops:
  0.6 80.7 %shard_map.93 = (f32[2,6,64,128]{3,2,1,0:T(8,128)}, f32[2,6,64,128]{3,2,1,0:T(8,128)}, f32[2,6,64,128]{3,2,1,0:T(8,128)}, f32[2,4,64,64]{3,2,1,0:T(8,128)}) custom-call(s32[2]{0:T(128)} %len_ref.1, bf16[2,6,64,128]{3,2,1,0:T(8,128)(2,1)} %q_ref.1, bf16[2,6,64,128]{3,2,1,0:T(8,128)(2,1)} %k_ref.1, bf16[2,6,64,128]{3,2,1,0:T(8,128)(2,1)} %v_ref.1, ...), custom_call_target="tpu_custom_call" | custom-call | flops 8000000000 | bytes 4000000 | tf_op jit(solution)/shard_map/pallas_call | solution.py:342
  81.3 0.0 copy-start.1
  81.3 1.8 %copy.14 = f32[2,6,64,128]{3,2,1,0:T(8,128)} copy(f32[2,6,64,128]{3,2,1,0:T(8,128)} %get-tuple-element.8) | data formatting | bytes 786432
  83.2 0.0 copy-done.1
  83.2 0.0 copy-start
  83.2 0.7 copy.15
  83.9 0.4 copy-done
  84.3 0.0 copy-start.2
  84.3 0.7 copy.16
  85.1 0.3 copy-done.2
  85.4 0.7 copy.17
Async XLA Ops:
  81.3 1.8 %copy-start.1 = (f32[2,6,64,128]{3,2,1,0:T(8,128)S(1)}, f32[2,6,64,128]{3,2,1,0:T(8,128)}, u32[]{:S(2)}) copy-start(f32[2,6,64,128]{3,2,1,0:T(8,128)} %get-tuple-element.9) | copy-start | bytes 1179652
  83.2 1.1 %copy-start = (f32[2,6,64,128]{3,2,1,0:T(8,128)S(1)}, f32[2,6,64,128]{3,2,1,0:T(8,128)}, u32[]{:S(2)}) copy-start(f32[2,6,64,128]{3,2,1,0:T(8,128)} %get-tuple-element.10) | copy-start | bytes 1179652
  84.3 1.1 %copy-start.2 = (f32[2,4,64,64]{3,2,1,0:T(8,128)S(1)}, f32[2,4,64,64]{3,2,1,0:T(8,128)}, u32[]{:S(2)}) copy-start(f32[2,4,64,64]{3,2,1,0:T(8,128)} %get-tuple-element.11) | copy-start | bytes 393220

commit v3 on v2

v3 whole, which is shorter than its diff:
```python
import jax
import jax.numpy as jnp
from jax import lax
from jax.experimental import pallas as pl
from jax.experimental.pallas import tpu as pltpu
from jax.sharding import PartitionSpec as P

H = 4
HD = 32
SEQ = 1024
NZ = 8
BLK = 64
HALF = SEQ // 2
NU = 3
NCHIP = 8
B = 256
NJ = HALF // B
R = 16
SUB = B // 2
LOG2E = 1.4426950408889634
SCALE = HD**-0.5
F32 = jnp.float32
BF16 = jnp.bfloat16
MESH = pl.DeviceIdType.MESH


def nn(a, b):
    return lax.dot_general(a, b, (((1,), (0,)), ((), ())), preferred_element_type=F32)


def wait_for(ref, sem):
    pltpu.make_async_copy(ref, ref, sem).wait()


def send(src, dst, send_sem, recv_sem, where):
    pltpu.make_async_remote_copy(
        src_ref=src,
        dst_ref=dst,
        send_sem=send_sem,
        recv_sem=recv_sem,
        device_id=where,
        device_id_type=MESH,
    ).start()


def at(index, size):
    return pl.ds(pl.multiple_of(index * size, size), size)


def kernel(
    len_ref, q_ref, k_ref, v_ref, g_ref, bias_ref,
    gq, gkv, fin,
    tsend, kv, qd, bias_full, b2, kvt, qdt, lhs, rhs, s_ref, dp_ref, ph, dsh, acc, dq, g32,
    psend, precv, gqsend, gkvsend, db, sib, rsend, red, fsend, own_fin,
    kv_ss, kv_rs, qd_ss, qd_rs, fw_ss, fw_rs, b1_ss, b1_rs, b1_ls, b2_ss, b2_rs, b3_ss, b3_rs,
    p_ss, p_rs, gq_ss, gq_rs, gk_ss, gk_rs, a_ss, a_rs, r_ss, r_rs, f_ss, f_rs, l_ss, l_rs,
):
    row = lax.axis_index("row")
    me = lax.axis_index("col")
    z = me % NZ
    yh = me // NZ
    chip = row // 2
    core = row % 2
    sibling = {"row": row + 1 - 2 * core}
    partner = {"col": (1 - yh) * NZ + z}
    others = [lax.rem(z + o, NZ) for o in range(1, NZ)]
    chips = [lax.rem(chip + o, NCHIP) for o in range(1, NCHIP)]

    def along_z(to):
        return {"col": yh * NZ + to}

    def along_row(to):
        return {"row": 2 * to + core}

    barrier = pltpu.get_barrier_semaphore()
    everyone = [along_z(to) for to in others] + [along_row(to) for to in chips] + [sibling, partner]
    for where in everyone:
        pl.semaphore_signal(barrier, inc=1, device_id=where, device_id_type=MESH)

    lane_block = lax.broadcasted_iota(jnp.int32, (BLK, 128), 1) // HD

    def lanes_from(parts):
        out = None
        for a, (x, b) in enumerate(parts):
            d = (a - b) % 4
            x = x if d == 0 else pltpu.roll(x, d * HD, 1)
            out = x if out is None else jnp.where(lane_block == a, x, out)
        return out

    def pack(u):
        for c in range(2):
            for kind, refs in enumerate(((k_ref, v_ref), (q_ref, g_ref))):
                arrays = [ref[c, 2 * u + e].astype(F32) for e in range(2) for ref in refs]
                for h in range(H):
                    tsend[u, kind, c * H + h] = lanes_from([(x, h) for x in arrays]).astype(BF16)
        kv[u, at(me, BLK), :] = tsend[u, 0, z]
        qd[u, at(z, BLK), :] = tsend[u, 1, z]

    def send_pack(u):
        for to in others:
            send(tsend.at[u, 0, to], kv.at[u, at(me, BLK)], kv_ss.at[u], kv_rs.at[u], along_z(to))
        for to in others:
            send(tsend.at[u, 1, to], qd.at[u, at(z, BLK)], qd_ss.at[u], qd_rs.at[u], along_z(to))

    def forward(u):
        wait_for(kv.at[u, pl.ds(0, BLK * (NZ - 1))], kv_rs.at[u])
        mine = kv.at[u, at(yh, HALF)]
        send(mine, mine, fw_ss.at[u], fw_rs.at[u], partner)

    my_rows = pl.ds(pl.multiple_of(core * 32 + (chip // 4) * 16, 16), 16)
    my_lanes = at(chip % 4, 256)

    def bias_to_chips(jb):
        mine = bias_full.at[pl.ds(jb * 4, 4), my_rows, my_lanes]
        for to in chips:
            send(mine, mine, b2_ss.at[jb], b2_rs.at[jb], along_row(to))

    def bias_to_sibling(jb):
        wait_for(bias_full.at[pl.ds(0, 7), :, pl.ds(0, 256)], b2_rs.at[jb])
        mine = bias_full.at[pl.ds(jb * 4, 4), at(core, 32)]
        send(mine, mine, b3_ss.at[jb], b3_rs.at[jb], sibling)

    pack(0)
    pl.semaphore_wait(barrier, len(everyone))
    for to in others:
        send(
            bias_ref.at[to // H, to % H, my_rows, my_lanes],
            bias_full.at[z, my_rows, my_lanes],
            b1_ss,
            b1_rs,
            along_z(to),
        )
    own = pltpu.make_async_copy(
        bias_ref.at[z // H, z % H, my_rows, my_lanes], bias_full.at[z, my_rows, my_lanes], b1_ls
    )
    own.start()
    send_pack(0)
    pack(1)
    own.wait()
    wait_for(bias_full.at[pl.ds(0, NZ - 1), pl.ds(0, 16), pl.ds(0, 256)], b1_rs)
    bias_to_chips(0)
    bias_to_chips(1)
    send_pack(1)
    forward(0)
    pack(2)
    send_pack(2)
    bias_to_sibling(0)
    n = len_ref[z // H]
    db[...] = jnp.zeros_like(db)

    def mask_bias(jb):
        col = lax.broadcasted_iota(jnp.int32, (R, SEQ), 1)
        for c in range(B // R):
            x = bias_full[jb * 4 + c // 4, pl.ds((c % 4) * R, R), :].astype(F32)
            b2[pl.ds(pl.multiple_of(jb * B + c * R, R), R), :] = jnp.where(col < n, x * LOG2E, -1e30)

    def prep(u):
        wait_for(qd.at[u, pl.ds(0, BLK * (NZ - 1))], qd_rs.at[u])
        x = qd[u]
        qdt[...] = x.T
        block = lax.broadcasted_iota(jnp.int32, x.shape, 1) // HD
        for b in range(4):
            lhs[b] = jnp.where(block == b, x, jnp.zeros_like(x))
        wait_for(kv.at[u, pl.ds(0, HALF)], fw_rs.at[u])
        x = kv[u]
        kvt[...] = x.T
        block = lax.broadcasted_iota(jnp.int32, x.shape, 1) // HD
        for e in range(2):
            rhs[e] = jnp.where(block == 2 * e, x, jnp.zeros_like(x))
        acc[...] = jnp.zeros_like(acc)
        dq[...] = jnp.zeros_like(dq)

    def tile(jb, e):
        j0 = pl.multiple_of(jb * B, B)
        rows = pl.ds(j0, B)
        keys = kvt[...]
        s_ref[...] = nn(lhs[2 * e, rows, :], keys)
        dp_ref[...] = nn(lhs[2 * e + 1, rows, :], keys)
        for c in range(B // R):
            r = pl.ds(c * R, R)
            jr = pl.ds(pl.multiple_of(j0 + c * R, R), R)
            s = s_ref[r, :] * (SCALE * LOG2E) + b2[jr, :]
            m = jnp.max(s, axis=1, keepdims=True)
            w = jnp.exp2(s - m)
            dp = dp_ref[r, :]
            rl = 1.0 / jnp.sum(w, axis=1, keepdims=True)
            delta = jnp.sum(w * dp, axis=1, keepdims=True) * rl
            pr = w * rl
            ds = pr * (dp - delta)
            ph[r, :] = pr.astype(BF16)
            dsh[r, :] = ds.astype(BF16)
            db[jr, :] += ds
        dsv = dsh[...]
        dq[rows, :] += nn(dsv, rhs[e])
        k_rows = pl.ds(pl.multiple_of(e * 64, 64), HD)
        v_rows = pl.ds(pl.multiple_of(e * 64 + HD, HD), HD)
        acc[k_rows, :] += nn(qdt[k_rows, rows], dsv)
        acc[v_rows, :] += nn(qdt[v_rows, rows], ph[...])

    def finish(u):
        even = (lax.broadcasted_iota(jnp.int32, (SEQ, 128), 1) // HD) % 2 == 0
        g = acc[...].T
        g32[...] = jnp.where(even, g * SCALE, g)
        psend[u] = g32[at(1 - yh, HALF), :].astype(BF16)
        send(psend.at[u], precv.at[u], p_ss.at[u], p_rs.at[u], partner)
        x = (dq[...] * SCALE).reshape(NZ, BLK, 128)
        even = (lax.broadcasted_iota(jnp.int32, (NZ, 32, 128), 2) // HD) % 2 == 0
        gqsend[u] = jnp.where(even, x[:, :32], pltpu.roll(x[:, 32:], HD, 2)).astype(BF16)
        gq[u, z] = gqsend[u, z]
        for to in others:
            send(gqsend.at[u, to], gq.at[u, z], gq_ss.at[u], gq_rs.at[u], along_z(to))

    def combine(u):
        wait_for(precv.at[u], p_rs.at[u])
        g = g32[at(yh, HALF), :] + precv[u].astype(F32)
        gkvsend[u] = g.astype(BF16).reshape(NZ, BLK, 128)
        gkv[u, z] = gkvsend[u, z]
        for to in others:
            send(gkvsend.at[u, to], gkv.at[u, z], gk_ss.at[u], gk_rs.at[u], along_z(to))

    def db_to_sibling(jb):
        theirs = db.at[pl.ds(pl.multiple_of(jb * B + (1 - core) * SUB, SUB), SUB)]
        send(theirs, sib.at[jb], a_ss.at[jb], a_rs.at[jb], sibling)

    def db_over_row(jb):
        wait_for(sib.at[jb], a_rs.at[jb])
        mine = pl.ds(pl.multiple_of(jb * B + core * SUB, SUB), SUB)
        for o in range(NCHIP):
            lanes = pl.ds(o * 128, 128)
            rsend[jb, o] = (db[mine, lanes] + sib[jb, :, lanes]).astype(BF16)
        red[jb, chip] = rsend[jb, chip]
        for to in chips:
            send(rsend.at[jb, to], red.at[jb, chip], r_ss.at[jb], r_rs.at[jb], along_row(to))

    def db_to_owner(jb):
        wait_for(red.at[jb, pl.ds(0, NCHIP - 1)], r_rs.at[jb])
        total = red[jb, 0].astype(F32)
        for o in range(1, NCHIP):
            total = total + red[jb, o].astype(F32)
        for e in range(2):
            to = jb * 4 + core * 2 + e
            fsend[jb * 2 + e] = total[e * BLK : (e + 1) * BLK]

            @pl.when(to == z)
            def _():
                fin[z] = fsend[jb * 2 + e]

            @pl.when(to != z)
            def _():
                send(fsend.at[jb * 2 + e], fin.at[z], f_ss, f_rs, along_z(to))

    @pl.loop(0, NU * 4)
    def _(it):
        u = it // 4
        jb = (it // 2) % 2
        e = it % 2

        @pl.when(it % 4 == 0)
        def _():
            prep(u)

        @pl.when((u == 0) & (e == 0))
        def _():
            wait_for(bias_full.at[pl.ds(0, 4), pl.ds(0, 32)], b3_rs.at[jb])
            mask_bias(jb)

        @pl.when(it == 1)
        def _():
            bias_to_sibling(1)

        @pl.when((it % 4 == 1) & (u < NU - 1))
        def _():
            forward(u + 1)

        @pl.when((it % 4 == 1) & (u > 0))
        def _():
            combine(u - 1)

        tile(jb, e)

        @pl.when((u == NU - 1) & (e == 1))
        def _():
            db_to_sibling(jb)

        @pl.when(it == NU * 4 - 2)
        def _():
            db_over_row(0)

        @pl.when(it % 4 == 3)
        def _():
            finish(u)

    db_over_row(1)
    db_to_owner(0)
    combine(NU - 1)
    db_to_owner(1)
    owner = (z // 2) % 2 == core

    @pl.when(owner)
    def _():
        wait_for(fin.at[pl.ds(0, NZ - 1)], f_rs)
        own_fin[...] = fin[...]
        send(own_fin, fin, l_ss, l_rs, sibling)
        wait_for(own_fin, l_ss)
        wait_for(fsend.at[pl.ds(0, 3)], f_ss)

    @pl.when(jnp.logical_not(owner))
    def _():
        wait_for(fin, l_rs)
        wait_for(fsend, f_ss)

    wait_for(bias_full.at[pl.ds(0, NZ - 1), pl.ds(0, 16), pl.ds(0, 256)], b1_ss)
    for u in range(NU):
        wait_for(gq.at[u, pl.ds(0, NZ - 1)], gq_rs.at[u])
        wait_for(gkv.at[u, pl.ds(0, NZ - 1)], gk_rs.at[u])
        wait_for(gq.at[u, pl.ds(0, NZ - 1)], gq_ss.at[u])
        wait_for(gkv.at[u, pl.ds(0, NZ - 1)], gk_ss.at[u])
        wait_for(kv.at[u, pl.ds(0, BLK * (NZ - 1))], kv_ss.at[u])
        wait_for(qd.at[u, pl.ds(0, BLK * (NZ - 1))], qd_ss.at[u])
        wait_for(kv.at[u, pl.ds(0, HALF)], fw_ss.at[u])
        wait_for(psend.at[u], p_ss.at[u])
    for jb in range(NJ):
        wait_for(bias_full.at[pl.ds(0, 7), :, pl.ds(0, 256)], b2_ss.at[jb])
        wait_for(bias_full.at[pl.ds(0, 4), pl.ds(0, 32)], b3_ss.at[jb])
        wait_for(sib.at[jb], a_ss.at[jb])
        wait_for(red.at[jb, pl.ds(0, NCHIP - 1)], r_ss.at[jb])


def unpack(core_ref, gq, gkv, fin, dq_out, dk_out, dv_out, db_out):
    lane_block = lax.broadcasted_iota(jnp.int32, (BLK, 128), 1) // HD

    def lanes_from(parts):
        out = None
        for h, (x, b) in enumerate(parts):
            d = (h - b) % 4
            x = x if d == 0 else pltpu.roll(x, d * HD, 1)
            out = x if out is None else jnp.where(lane_block == h, x, out)
        return out

    for u in range(NU):
        folded = [gq[u, h].astype(F32) for h in range(H)]
        folded = [jnp.concatenate([x, pltpu.roll(x, 128 - HD, 1)], axis=0) for x in folded]
        pairs = [gkv[u, h].astype(F32) for h in range(H)]
        for e in range(2):
            dq_out[0, 2 * u + e] = lanes_from([(x, 2 * e) for x in folded])
            dk_out[0, 2 * u + e] = lanes_from([(x, 2 * e) for x in pairs])
            dv_out[0, 2 * u + e] = lanes_from([(x, 2 * e + 1) for x in pairs])
    for h in range(H):
        x = fin[h]
        x = jnp.where(core_ref[0] == 0, x, pltpu.roll(x, 64, 1))
        db_out[0, h] = x[:, 0:64]


def per_device(query, key, value, grad_out, pair_bias, crop_lengths):
    V = pltpu.VMEM
    D = pltpu.SemaphoreType.DMA
    vm = pl.BlockSpec(memory_space=V)
    gq, gkv, fin = pl.pallas_call(
        kernel,
        out_shape=(
            jax.ShapeDtypeStruct((NU, NZ, 32, 128), BF16),
            jax.ShapeDtypeStruct((NU, NZ, BLK, 128), BF16),
            jax.ShapeDtypeStruct((NZ, BLK, 128), F32),
        ),
        in_specs=[pl.BlockSpec(memory_space=pltpu.SMEM)] + [vm] * 5,
        out_specs=(vm, vm, vm),
        scratch_shapes=[
            V((NU, 2, NZ, BLK, 128), BF16),
            V((NU, SEQ, 128), BF16),
            V((NU, HALF, 128), BF16),
            V((NZ, BLK, SEQ), BF16),
            V((HALF, SEQ), F32),
            V((128, SEQ), BF16),
            V((128, HALF), BF16),
            V((4, HALF, 128), BF16),
            V((2, SEQ, 128), BF16),
            V((B, SEQ), F32),
            V((B, SEQ), F32),
            V((B, SEQ), BF16),
            V((B, SEQ), BF16),
            V((128, SEQ), F32),
            V((HALF, 128), F32),
            V((SEQ, 128), F32),
            V((NU, HALF, 128), BF16),
            V((NU, HALF, 128), BF16),
            V((NU, NZ, 32, 128), BF16),
            V((NU, NZ, BLK, 128), BF16),
            V((HALF, SEQ), F32),
            V((NJ, SUB, SEQ), F32),
            V((NJ, NCHIP, SUB, 128), BF16),
            V((NJ, NCHIP, SUB, 128), BF16),
            V((4, BLK, 128), F32),
            V((NZ, BLK, 128), F32),
        ]
        + [D((NU,))] * 6
        + [D] * 3
        + [D((NJ,))] * 4
        + [D((NU,))] * 6
        + [D((NJ,))] * 4
        + [D] * 4,
        compiler_params=pltpu.CompilerParams(
            vmem_limit_bytes=60 * 2**20, collective_id=0, has_side_effects=True
        ),
        cost_estimate=pl.CostEstimate(flops=8 * 10**9, bytes_accessed=4 * 10**6, transcendentals=3 * 2**20),
    )(crop_lengths, query, key, value, grad_out, pair_bias)
    grad = jax.ShapeDtypeStruct(query.shape, F32)
    spec = pl.BlockSpec((1, 6, BLK, 128), lambda c: (c, 0, 0, 0))
    return pl.pallas_call(
        unpack,
        grid=(2,),
        out_shape=(grad, grad, grad, jax.ShapeDtypeStruct((2, H, BLK, BLK), F32)),
        in_specs=[
            pl.BlockSpec(memory_space=pltpu.SMEM),
            pl.BlockSpec((NU, H, 32, 128), lambda c: (0, c, 0, 0)),
            pl.BlockSpec((NU, H, BLK, 128), lambda c: (0, c, 0, 0)),
            pl.BlockSpec((H, BLK, 128), lambda c: (c, 0, 0)),
        ],
        out_specs=(spec, spec, spec, pl.BlockSpec((1, H, BLK, BLK), lambda c: (c, 0, 0, 0))),
    )(lax.rem(lax.axis_index("row"), 2)[None], gq, gkv, fin)


def solution(mesh):
    spec = P(None, "row", "col", None)
    return jax.shard_map(
        per_device,
        mesh=mesh,
        in_specs=(spec, spec, spec, spec, P(None, None, "col", None), P()),
        out_specs=(spec, spec, spec, P(None, None, "col", "row")),
        check_vma=False,
    )
```

time: 86.3 us -> 71.2 us (0.83)
  the two profiles are of different devices: /device:TPU:17 before, /device:TPU:1 now
where the time goes in v3:
time: 71.2 us; the launch traced here: 71.1 us
  Pallas kernels  70.4 us (99%)
    pallas_call x1, Pallas kernels, per_device(): pl.pallas_call(kernel, out_shape=(jax.ShapeDtypeStruct((NU, NZ, 32, 128),...  67.6 us
    pallas_call x1, Pallas kernels, per_device(): pl.pallas_call(unpack, grid=(2,), out_shape=(grad, grad, grad, jax.ShapeD...  2.83 us

profile of v3, /device:TPU:1, one launch (start us, length us, event | category | flops | bytes accessed | tf_op | source)
XLA Modules:
  0.0 71.1 jit_solution(1876264253629837657)
XLA Ops:
  0.6 67.6 %shard_map.93 = (bf16[3,8,32,128]{3,2,1,0:T(8,128)(2,1)}, bf16[3,8,64,128]{3,2,1,0:T(8,128)(2,1)}, f32[8,64,128]{2,1,0:T(8,128)}) custom-call(s32[2]{0:T(128)} %len_ref.1, bf16[2,6,64,128]{3,2,1,0:T(8,128)(2,1)} %q_ref.1, bf16[2,6,64,128]{3,2,1,0:T(8,128)(2,1)} %k_ref.1, bf16[2,6,64,128]{3,2,1,0:T(8,128)(2,1)} %v_ref.1, bf16[2,6,64,128]{3,2,1,0:T(8,128)(2,1)} %g_ref.1, ...), custom_call_target="tpu_custom_call" | custom-call | flops 8000000000 | bytes 4000000 | tf_op jit(solution)/shard_map/pallas_call | solution.py:358
  68.3 2.8 %shard_map.94 = (f32[2,6,64,128]{3,2,1,0:T(8,128)}, f32[2,6,64,128]{3,2,1,0:T(8,128)}, f32[2,6,64,128]{3,2,1,0:T(8,128)}, f32[2,4,64,64]{3,2,1,0:T(8,128)}) custom-call(s32[1]{0:T(128)} %bitcast.core_ref, bf16[3,8,32,128]{3,2,1,0:T(8,128)(2,1)} %get-tuple-element.7.gq, bf16[3,8,64,128]{3,2,1,0:T(8,128)(2,1)} %get-tuple-element.8.gkv, ...), custom_call_target="tpu_custom_call" | custom-call | tf_op jit(solution)/shard_map/pallas_call | solution.py:408

commit v4 on v3

v4 whole, which is shorter than its diff:
```python
import jax
import jax.numpy as jnp
from jax import lax
from jax.experimental import pallas as pl
from jax.experimental.pallas import tpu as pltpu
from jax.sharding import PartitionSpec as P

H = 4
HD = 32
SEQ = 1024
NZ = 8
BLK = 64
HALF = SEQ // 2
NU = 3
NP = 2 * NU
NCHIP = 8
B = 256
NJ = HALF // B
R = 16
SUB = B // 2
LOG2E = 1.4426950408889634
SCALE = HD**-0.5
F32 = jnp.float32
BF16 = jnp.bfloat16
MESH = pl.DeviceIdType.MESH


def nn(a, b):
    return lax.dot_general(a, b, (((1,), (0,)), ((), ())), preferred_element_type=F32)


def wait_for(ref, sem):
    pltpu.make_async_copy(ref, ref, sem).wait()


def send(src, dst, send_sem, recv_sem, where):
    pltpu.make_async_remote_copy(
        src_ref=src,
        dst_ref=dst,
        send_sem=send_sem,
        recv_sem=recv_sem,
        device_id=where,
        device_id_type=MESH,
    ).start()


def at(index, size):
    return pl.ds(pl.multiple_of(index * size, size), size)


def kernel(
    len_ref, q_ref, k_ref, v_ref, g_ref, bias_ref,
    gq, gkv, fin,
    tsend, kv, qd, bias_full, b2, kvt, qdt, lhs, s_ref, dp_ref, ph, dsh, acc, dqt, g32,
    psend, precv, gqsend, gkvsend, db, sib, rsend, red, fsend,
    kv_ss, kv_rs, qd_ss, qd_rs, fw_ss, fw_rs, b1_ss, b1_rs, b1_ls, b2_ss, b2_rs, by_ss, by_rs, b3_ss, b3_rs,
    p_ss, p_rs, gq_ss, gq_rs, gk_ss, gk_rs, a_ss, a_rs, r_ss, r_rs, f_ss, f_rs,
):
    row = lax.axis_index("row")
    me = lax.axis_index("col")
    z = me % NZ
    yh = me // NZ
    chip = row // 2
    core = row % 2
    sibling = {"row": row + 1 - 2 * core}
    partner = {"col": (1 - yh) * NZ + z}
    others = [lax.rem(z + o, NZ) for o in range(1, NZ)]
    chips = [lax.rem(chip + o, NCHIP) for o in range(1, NCHIP)]

    def along_z(to):
        return {"col": yh * NZ + to}

    def along_row(to):
        return {"row": 2 * to + core}

    barrier = pltpu.get_barrier_semaphore()
    everyone = [along_z(to) for to in others] + [along_row(to) for to in chips] + [sibling, partner]
    everyone += [along_z(to) | sibling for to in others]
    for where in everyone:
        pl.semaphore_signal(barrier, inc=1, device_id=where, device_id_type=MESH)

    lane_block = lax.broadcasted_iota(jnp.int32, (BLK, 128), 1) // HD

    def lanes_from(parts):
        out = None
        for a, (x, b) in enumerate(parts):
            d = (a - b) % 4
            x = x if d == 0 else pltpu.roll(x, d * HD, 1)
            out = x if out is None else jnp.where(lane_block == a, x, out)
        return out

    def pack(u):
        for c in range(2):
            for kind, refs in enumerate(((k_ref, v_ref), (q_ref, g_ref))):
                arrays = [ref[c, 2 * u + e].astype(F32) for e in range(2) for ref in refs]
                for h in range(H):
                    tsend[u, kind, c * H + h] = lanes_from([(x, h) for x in arrays]).astype(BF16)
        kv[u, at(me, BLK), :] = tsend[u, 0, z]
        qd[u, at(z, BLK), :] = tsend[u, 1, z]

    def send_kv(u):
        for to in others:
            send(tsend.at[u, 0, to], kv.at[u, at(me, BLK)], kv_ss.at[u], kv_rs.at[u], along_z(to))

    def send_qd(u):
        for to in others:
            send(tsend.at[u, 1, to], qd.at[u, at(z, BLK)], qd_ss.at[u], qd_rs.at[u], along_z(to))

    def forward(u):
        wait_for(kv.at[u, pl.ds(0, BLK * (NZ - 1))], kv_rs.at[u])
        mine = kv.at[u, at(yh, HALF)]
        send(mine, mine, fw_ss.at[u], fw_rs.at[u], partner)

    ylo = chip // 4
    my_rows = pl.ds(pl.multiple_of(core * 32 + ylo * 16, 16), 16)
    their_rows = pl.ds(pl.multiple_of(core * 32 + (1 - ylo) * 16, 16), 16)
    my_lanes = at(chip % 4, 256)
    x_chips = [ylo * 4 + (chip + o) % 4 for o in range(1, 4)]
    y_chip = (1 - ylo) * 4 + chip % 4

    def bias_to_chips(jb):
        mine = bias_full.at[pl.ds(jb * 4, 4), my_rows, my_lanes]
        send(mine, mine, by_ss.at[jb], by_rs.at[jb], along_row(y_chip))
        for to in x_chips:
            send(mine, mine, b2_ss.at[jb], b2_rs.at[jb], along_row(to))

    def bias_onward(jb):
        theirs = bias_full.at[pl.ds(jb * 4, 4), their_rows, my_lanes]
        wait_for(theirs, by_rs.at[jb])
        for to in x_chips:
            send(theirs, theirs, b2_ss.at[jb], b2_rs.at[jb], along_row(to))

    def bias_to_sibling(jb):
        wait_for(bias_full.at[pl.ds(0, 6), :, pl.ds(0, 256)], b2_rs.at[jb])
        mine = bias_full.at[pl.ds(jb * 4, 4), at(core, 32)]
        send(mine, mine, b3_ss.at[jb], b3_rs.at[jb], sibling)

    pack(0)
    pack(1)
    pl.semaphore_wait(barrier, len(everyone))
    for to in others:
        send(
            bias_ref.at[to // H, to % H, my_rows, my_lanes],
            bias_full.at[z, my_rows, my_lanes],
            b1_ss,
            b1_rs,
            along_z(to),
        )
    own = pltpu.make_async_copy(
        bias_ref.at[z // H, z % H, my_rows, my_lanes], bias_full.at[z, my_rows, my_lanes], b1_ls
    )
    own.start()
    send_kv(0)
    send_qd(0)
    own.wait()
    wait_for(bias_full.at[pl.ds(0, NZ - 1), pl.ds(0, 16), pl.ds(0, 256)], b1_rs)
    bias_to_chips(0)
    bias_to_chips(1)
    send_kv(1)
    send_qd(1)
    pack(2)
    send_kv(2)
    send_qd(2)
    bias_onward(0)
    bias_onward(1)
    forward(0)
    bias_to_sibling(0)
    n = len_ref[z // H]
    db[...] = jnp.zeros_like(db)

    def mask_bias(jb):
        col = lax.broadcasted_iota(jnp.int32, (R, SEQ), 1)
        for c in range(B // R):
            x = bias_full[jb * 4 + c // 4, pl.ds((c % 4) * R, R), :].astype(F32)
            b2[pl.ds(pl.multiple_of(jb * B + c * R, R), R), :] = jnp.where(col < n, x * LOG2E, -1e30)

    def prep(u):
        wait_for(qd.at[u, pl.ds(0, BLK * (NZ - 1))], qd_rs.at[u])
        x = qd[u]
        qdt[...] = x.T
        block = lax.broadcasted_iota(jnp.int32, x.shape, 1) // HD
        for b in range(4):
            lhs[b] = jnp.where(block == b, x, jnp.zeros_like(x))
        wait_for(kv.at[u, pl.ds(0, HALF)], fw_rs.at[u])
        x = kv[u]
        kvt[...] = x.T
        acc[...] = jnp.zeros_like(acc)
        dqt[...] = jnp.zeros_like(dqt)

    def tile(jb):
        j0 = pl.multiple_of(jb * B, B)
        rows = pl.ds(j0, B)
        keys = kvt[...]
        for e in range(2):
            s_ref[e] = nn(lhs[2 * e, rows, :], keys)
            dp_ref[e] = nn(lhs[2 * e + 1, rows, :], keys)
        for c in range(B // R):
            r = pl.ds(c * R, R)
            jr = pl.ds(pl.multiple_of(j0 + c * R, R), R)
            total = db[jr, :]
            for e in range(2):
                s = s_ref[e, r, :] * (SCALE * LOG2E) + b2[jr, :]
                m = jnp.max(s, axis=1, keepdims=True)
                w = jnp.exp2(s - m)
                dp = dp_ref[e, r, :]
                rl = 1.0 / jnp.sum(w, axis=1, keepdims=True)
                delta = jnp.sum(w * dp, axis=1, keepdims=True) * rl
                pr = w * rl
                ds = pr * (dp - delta)
                ph[e, r, :] = pr.astype(BF16)
                dsh[e, r, :] = ds.astype(BF16)
                total = total + ds
            db[jr, :] = total
        for e in range(2):
            dsv = dsh[e]
            first, second = pl.ds(e * 64, HD), pl.ds(e * 64 + HD, HD)
            dqt[pl.ds(e * HD, HD), rows] += lax.dot_general(
                kvt[first, :], dsv, (((1,), (1,)), ((), ())), preferred_element_type=F32
            )
            acc[first, :] += nn(qdt[first, rows], dsv)
            acc[second, :] += nn(qdt[second, rows], ph[e])

    def finish_kv(u):
        even = (lax.broadcasted_iota(jnp.int32, (SEQ, 128), 1) // HD) % 2 == 0
        g = acc[...].T
        g = jnp.where(even, g * SCALE, g).reshape(2 * NZ, BLK, 128)
        top, low = g[:, :32], g[:, 32:]
        lane = lax.broadcasted_iota(jnp.int32, top.shape, 2)
        g32[0] = jnp.where(lane < 64, top, pltpu.roll(low, 64, 2))
        g32[1] = jnp.where(lane < 64, pltpu.roll(top, 64, 2), low)
        for e in range(2):
            p = 2 * u + e
            psend[p] = g32[e, at(1 - yh, NZ)].astype(BF16)
            send(psend.at[p], precv.at[p], p_ss.at[p], p_rs.at[p], partner)

    def finish_q(u):
        x = jnp.concatenate([dqt[...] * SCALE, jnp.zeros_like(dqt)], axis=0).T
        x = x.reshape(NZ, BLK, 128)
        lane = lax.broadcasted_iota(jnp.int32, (NZ, 32, 128), 2)
        gqsend[u] = jnp.where(lane < 64, x[:, :32], pltpu.roll(x[:, 32:], 64, 2)).astype(BF16)
        gq[u, z] = gqsend[u, z]
        for to in others:
            send(gqsend.at[u, to], gq.at[u, z], gq_ss.at[u], gq_rs.at[u], along_z(to))

    def combine(p):
        wait_for(precv.at[p], p_rs.at[p])
        gkvsend[p] = (g32[p % 2, at(yh, NZ)] + precv[p].astype(F32)).astype(BF16)
        gkv[p, z] = gkvsend[p, z]
        for to in others:
            send(gkvsend.at[p, to], gkv.at[p, z], gk_ss.at[p], gk_rs.at[p], along_z(to))

    def db_to_sibling(jb):
        theirs = db.at[pl.ds(pl.multiple_of(jb * B + (1 - core) * SUB, SUB), SUB)]
        send(theirs, sib.at[jb], a_ss.at[jb], a_rs.at[jb], sibling)

    def db_over_row(jb):
        wait_for(sib.at[jb], a_rs.at[jb])
        mine = pl.ds(pl.multiple_of(jb * B + core * SUB, SUB), SUB)
        for o in range(NCHIP):
            lanes = pl.ds(o * 128, 128)
            rsend[jb, o] = (db[mine, lanes] + sib[jb, :, lanes]).astype(BF16)
        red[jb, chip] = rsend[jb, chip]
        for to in chips:
            send(rsend.at[jb, to], red.at[jb, chip], r_ss.at[jb], r_rs.at[jb], along_row(to))

    def db_to_owner(jb):
        wait_for(red.at[jb, pl.ds(0, NCHIP - 1)], r_rs.at[jb])
        total = red[jb, 0].astype(F32)
        for o in range(1, NCHIP):
            total = total + red[jb, o].astype(F32)
        lane = lax.broadcasted_iota(jnp.int32, (32, 128), 1)
        for e in range(2):
            to = jb * 4 + core * 2 + e
            top = total[e * BLK : e * BLK + 32]
            low = total[e * BLK + 32 : (e + 1) * BLK]
            fsend[jb * 4 + e * 2] = jnp.where(lane < 64, top, pltpu.roll(low, 64, 1))
            fsend[jb * 4 + e * 2 + 1] = jnp.where(lane < 64, pltpu.roll(top, 64, 1), low)
            for a in range(2):
                mine = (to == z) & (core == a)

                @pl.when(mine)
                def _():
                    fin[z] = fsend[jb * 4 + e * 2 + a]

                @pl.when(jnp.logical_not(mine))
                def _():
                    where = along_z(to) | {"row": 2 * chip + a}
                    send(fsend.at[jb * 4 + e * 2 + a], fin.at[z], f_ss, f_rs, where)

    @pl.loop(0, NP)
    def _(it):
        u = it // NJ
        jb = it % NJ

        @pl.when(jb == 0)
        def _():
            prep(u)

        @pl.when(u == 0)
        def _():
            @pl.when(jb == 0)
            def _():
                bias_to_sibling(1)

            wait_for(bias_full.at[pl.ds(0, 4), pl.ds(0, 32)], b3_rs.at[jb])
            mask_bias(jb)

        @pl.when((jb == 0) & (u < NU - 1))
        def _():
            forward(u + 1)

        @pl.when((jb == 1) & (u > 0))
        def _():
            combine(2 * u - 2)

        tile(jb)

        @pl.when(u == NU - 1)
        def _():
            db_to_sibling(jb)

        @pl.when(it == NP - 1)
        def _():
            db_over_row(0)

        @pl.when((jb == 1) & (u > 0))
        def _():
            combine(2 * u - 1)

        @pl.when(jb == 1)
        def _():
            finish_kv(u)
            finish_q(u)

    db_over_row(1)
    combine(NP - 2)
    db_to_owner(0)
    combine(NP - 1)
    db_to_owner(1)
    owner = (z // 2) % 2 == core

    @pl.when(owner)
    def _():
        wait_for(fin.at[pl.ds(0, NZ - 1)], f_rs)
        wait_for(fsend.at[pl.ds(0, NZ - 1)], f_ss)

    @pl.when(jnp.logical_not(owner))
    def _():
        wait_for(fin, f_rs)
        wait_for(fsend, f_ss)

    wait_for(bias_full.at[pl.ds(0, NZ - 1), pl.ds(0, 16), pl.ds(0, 256)], b1_ss)
    for u in range(NU):
        wait_for(gq.at[u, pl.ds(0, NZ - 1)], gq_rs.at[u])
        wait_for(gq.at[u, pl.ds(0, NZ - 1)], gq_ss.at[u])
        wait_for(kv.at[u, pl.ds(0, BLK * (NZ - 1))], kv_ss.at[u])
        wait_for(qd.at[u, pl.ds(0, BLK * (NZ - 1))], qd_ss.at[u])
        wait_for(kv.at[u, pl.ds(0, HALF)], fw_ss.at[u])
    for p in range(NP):
        wait_for(gkv.at[p, pl.ds(0, NZ - 1)], gk_rs.at[p])
        wait_for(gkv.at[p, pl.ds(0, NZ - 1)], gk_ss.at[p])
        wait_for(psend.at[p], p_ss.at[p])
    for jb in range(NJ):
        wait_for(bias_full.at[pl.ds(0, 6), :, pl.ds(0, 256)], b2_ss.at[jb])
        wait_for(bias_full.at[pl.ds(0, 4), pl.ds(0, 16), pl.ds(0, 256)], by_ss.at[jb])
        wait_for(bias_full.at[pl.ds(0, 4), pl.ds(0, 32)], b3_ss.at[jb])
        wait_for(sib.at[jb], a_ss.at[jb])
        wait_for(red.at[jb, pl.ds(0, NCHIP - 1)], r_ss.at[jb])


def unpack(gq, gkv, fin, dq_out, dk_out, dv_out, db_out):
    lane_block = lax.broadcasted_iota(jnp.int32, (BLK, 128), 1) // HD

    def lanes_from(parts):
        out = None
        for h, (x, b) in enumerate(parts):
            d = (h - b) % 4
            x = x if d == 0 else pltpu.roll(x, d * HD, 1)
            out = x if out is None else jnp.where(lane_block == h, x, out)
        return out

    def unfold(parts, lanes):
        parts = [x.astype(F32) for x in parts]
        return [jnp.concatenate([x, pltpu.roll(x, 128 - lanes, 1)], axis=0) for x in parts]

    for u in range(NU):
        folded = unfold([gq[u, h] for h in range(H)], 64)
        for e in range(2):
            pairs = unfold([gkv[2 * u + e, h] for h in range(H)], 64)
            dq_out[0, 2 * u + e] = lanes_from([(x, e) for x in folded])
            dk_out[0, 2 * u + e] = lanes_from([(x, 0) for x in pairs])
            dv_out[0, 2 * u + e] = lanes_from([(x, 1) for x in pairs])
    for h in range(H):
        x = fin[h]
        db_out[0, h, :32] = x[:, :64]
        db_out[0, h, 32:] = pltpu.roll(x, 64, 1)[:, :64]


def per_device(query, key, value, grad_out, pair_bias, crop_lengths):
    V = pltpu.VMEM
    D = pltpu.SemaphoreType.DMA
    vm = pl.BlockSpec(memory_space=V)
    gq, gkv, fin = pl.pallas_call(
        kernel,
        out_shape=(
            jax.ShapeDtypeStruct((NU, NZ, 32, 128), BF16),
            jax.ShapeDtypeStruct((NP, NZ, 32, 128), BF16),
            jax.ShapeDtypeStruct((NZ, 32, 128), F32),
        ),
        in_specs=[pl.BlockSpec(memory_space=pltpu.SMEM)] + [vm] * 5,
        out_specs=(vm, vm, vm),
        scratch_shapes=[
            V((NU, 2, NZ, BLK, 128), BF16),
            V((NU, SEQ, 128), BF16),
            V((NU, HALF, 128), BF16),
            V((NZ, BLK, SEQ), BF16),
            V((HALF, SEQ), F32),
            V((128, SEQ), BF16),
            V((128, HALF), BF16),
            V((4, HALF, 128), BF16),
            V((2, B, SEQ), F32),
            V((2, B, SEQ), F32),
            V((2, B, SEQ), BF16),
            V((2, B, SEQ), BF16),
            V((128, SEQ), F32),
            V((64, HALF), F32),
            V((2, 2 * NZ, 32, 128), F32),
            V((NP, NZ, 32, 128), BF16),
            V((NP, NZ, 32, 128), BF16),
            V((NU, NZ, 32, 128), BF16),
            V((NP, NZ, 32, 128), BF16),
            V((HALF, SEQ), F32),
            V((NJ, SUB, SEQ), F32),
            V((NJ, NCHIP, SUB, 128), BF16),
            V((NJ, NCHIP, SUB, 128), BF16),
            V((NZ, 32, 128), F32),
        ]
        + [D((NU,))] * 6
        + [D] * 3
        + [D((NJ,))] * 6
        + [D((NP,))] * 2
        + [D((NU,))] * 2
        + [D((NP,))] * 2
        + [D((NJ,))] * 4
        + [D] * 2,
        compiler_params=pltpu.CompilerParams(
            vmem_limit_bytes=60 * 2**20, collective_id=0, has_side_effects=True
        ),
        cost_estimate=pl.CostEstimate(flops=8 * 10**9, bytes_accessed=4 * 10**6, transcendentals=3 * 2**20),
    )(crop_lengths, query, key, value, grad_out, pair_bias)
    grad = jax.ShapeDtypeStruct(query.shape, F32)
    spec = pl.BlockSpec((1, 6, BLK, 128), lambda c: (c, 0, 0, 0))
    return pl.pallas_call(
        unpack,
        grid=(2,),
        out_shape=(grad, grad, grad, jax.ShapeDtypeStruct((2, H, BLK, BLK), F32)),
        in_specs=[
            pl.BlockSpec((NU, H, 32, 128), lambda c: (0, c, 0, 0)),
            pl.BlockSpec((NP, H, 32, 128), lambda c: (0, c, 0, 0)),
            pl.BlockSpec((H, 32, 128), lambda c: (c, 0, 0)),
        ],
        out_specs=(spec, spec, spec, pl.BlockSpec((1, H, BLK, BLK), lambda c: (c, 0, 0, 0))),
    )(gq, gkv, fin)


def solution(mesh):
    spec = P(None, "row", "col", None)
    return jax.shard_map(
        per_device,
        mesh=mesh,
        in_specs=(spec, spec, spec, spec, P(None, None, "col", None), P()),
        out_specs=(spec, spec, spec, P(None, None, "col", "row")),
        check_vma=False,
    )
```

time: 71.2 us -> 64.8 us (0.910)
  Pallas kernels: 70.4 us -> 64.1 us
    pallas_call x1, Pallas kernels: 67.6 us -> 61.1 us  [per_device(): pl.pallas_call(kernel, out_shape=(jax.ShapeDtypeStruct((NU, NZ, 32, 128),...]
where the time goes in v4:
time: 64.8 us; the launch traced here: 64.7 us
  Pallas kernels  64.1 us (99%)
    pallas_call x1, Pallas kernels, per_device(): pl.pallas_call(kernel, out_shape=(jax.ShapeDtypeStruct((NU, NZ, 32, 128),...  61.1 us
    pallas_call x1, Pallas kernels, per_device(): pl.pallas_call(unpack, grid=(2,), out_shape=(grad, grad, grad, jax.ShapeD...  2.95 us

profile of v4, /device:TPU:1, one launch (start us, length us, event | category | flops | bytes accessed | tf_op | source)
XLA Modules:
  0.0 64.7 jit_solution(16321323845230222944)
XLA Ops:
  0.6 61.1 %shard_map.93 = (bf16[3,8,32,128]{3,2,1,0:T(8,128)(2,1)}, bf16[6,8,32,128]{3,2,1,0:T(8,128)(2,1)}, f32[8,32,128]{2,1,0:T(8,128)}) custom-call(s32[2]{0:T(128)} %len_ref.1, bf16[2,6,64,128]{3,2,1,0:T(8,128)(2,1)} %q_ref.1, bf16[2,6,64,128]{3,2,1,0:T(8,128)(2,1)} %k_ref.1, bf16[2,6,64,128]{3,2,1,0:T(8,128)(2,1)} %v_ref.1, bf16[2,6,64,128]{3,2,1,0:T(8,128)(2,1)} %g_ref.1, ...), custom_call_target="tpu_custom_call" | custom-call | flops 8000000000 | bytes 4000000 | tf_op jit(solution)/shard_map/pallas_call | solution.py:403
  61.8 2.9 %shard_map.94 = (f32[2,6,64,128]{3,2,1,0:T(8,128)}, f32[2,6,64,128]{3,2,1,0:T(8,128)}, f32[2,6,64,128]{3,2,1,0:T(8,128)}, f32[2,4,64,64]{3,2,1,0:T(8,128)}) custom-call(bf16[3,8,32,128]{3,2,1,0:T(8,128)(2,1)} %get-tuple-element.7.gq, bf16[6,8,32,128]{3,2,1,0:T(8,128)(2,1)} %get-tuple-element.8.gkv, f32[8,32,128]{2,1,0:T(8,128)} %get-tuple-element.9.fin), custom_call_target="tpu_custom_call" | custom-call | tf_op jit(solution)/shard_map/pallas_call | solution.py:453

commit v5 on v4

--- a/solution.py
+++ b/solution.py
@@ -49,12 +49,12 @@
 
 
 def kernel(
-    len_ref, q_ref, k_ref, v_ref, g_ref, bias_ref,
+    len_ref, q_hbm, k_hbm, v_hbm, g_hbm, bias_ref,
     gq, gkv, fin,
-    tsend, kv, qd, bias_full, b2, kvt, qdt, lhs, s_ref, dp_ref, ph, dsh, acc, dqt, g32,
-    psend, precv, gqsend, gkvsend, db, sib, rsend, red, fsend,
+    q_ref, k_ref, v_ref, g_ref, tsend, kv, qd, bias_full, b2, kvt, qdt, s_ref, dp_ref, ph, dsh, acc, dqt, g32,
+    psend, precv, gqsend, gkvsend, db, sib, rsend, red, redx, ysend, yrecv, fsend,
     kv_ss, kv_rs, qd_ss, qd_rs, fw_ss, fw_rs, b1_ss, b1_rs, b1_ls, b2_ss, b2_rs, by_ss, by_rs, b3_ss, b3_rs,
-    p_ss, p_rs, gq_ss, gq_rs, gk_ss, gk_rs, a_ss, a_rs, r_ss, r_rs, f_ss, f_rs,
+    p_ss, p_rs, gq_ss, gq_rs, gk_ss, gk_rs, a_ss, a_rs, r_ss, r_rs, f_ss, f_rs, y_ss, y_rs, in_ls,
 ):
     row = lax.axis_index("row")
     me = lax.axis_index("col")
@@ -78,6 +78,12 @@
     everyone += [along_z(to) | sibling for to in others]
     for where in everyone:
         pl.semaphore_signal(barrier, inc=1, device_id=where, device_id_type=MESH)
+    loads = [
+        pltpu.make_async_copy(src, dst, in_ls.at[i])
+        for i, (src, dst) in enumerate(((k_hbm, k_ref), (v_hbm, v_ref), (q_hbm, q_ref), (g_hbm, g_ref)))
+    ]
+    for load in loads:
+        load.start()
 
     lane_block = lax.broadcasted_iota(jnp.int32, (BLK, 128), 1) // HD
 
@@ -135,6 +141,8 @@
         mine = bias_full.at[pl.ds(jb * 4, 4), at(core, 32)]
         send(mine, mine, b3_ss.at[jb], b3_rs.at[jb], sibling)
 
+    for load in loads:
+        load.wait()
     pack(0)
     pack(1)
     pl.semaphore_wait(barrier, len(everyone))
@@ -157,9 +165,9 @@
     bias_to_chips(0)
     bias_to_chips(1)
     send_kv(1)
-    send_qd(1)
     pack(2)
     send_kv(2)
+    send_qd(1)
     send_qd(2)
     bias_onward(0)
     bias_onward(1)
@@ -178,22 +186,19 @@
         wait_for(qd.at[u, pl.ds(0, BLK * (NZ - 1))], qd_rs.at[u])
         x = qd[u]
         qdt[...] = x.T
-        block = lax.broadcasted_iota(jnp.int32, x.shape, 1) // HD
-        for b in range(4):
-            lhs[b] = jnp.where(block == b, x, jnp.zeros_like(x))
         wait_for(kv.at[u, pl.ds(0, HALF)], fw_rs.at[u])
         x = kv[u]
         kvt[...] = x.T
         acc[...] = jnp.zeros_like(acc)
         dqt[...] = jnp.zeros_like(dqt)
 
-    def tile(jb):
+    def tile(u, jb):
         j0 = pl.multiple_of(jb * B, B)
         rows = pl.ds(j0, B)
-        keys = kvt[...]
         for e in range(2):
-            s_ref[e] = nn(lhs[2 * e, rows, :], keys)
-            dp_ref[e] = nn(lhs[2 * e + 1, rows, :], keys)
+            first, second = pl.ds(e * 64, HD), pl.ds(e * 64 + HD, HD)
+            s_ref[e] = nn(qd[u, rows, first], kvt[first, :])
+            dp_ref[e] = nn(qd[u, rows, second], kvt[second, :])
         for c in range(B // R):
             r = pl.ds(c * R, R)
             jr = pl.ds(pl.multiple_of(j0 + c * R, R), R)
@@ -259,15 +264,37 @@
         for o in range(NCHIP):
             lanes = pl.ds(o * 128, 128)
             rsend[jb, o] = (db[mine, lanes] + sib[jb, :, lanes]).astype(BF16)
-        red[jb, chip] = rsend[jb, chip]
-        for to in chips:
-            send(rsend.at[jb, to], red.at[jb, chip], r_ss.at[jb], r_rs.at[jb], along_row(to))
+        if jb == 0:
+            redx[0, chip % 4] = rsend[0, chip]
+            redx[1, chip % 4] = rsend[0, y_chip]
+            for to in x_chips:
+                send(rsend.at[0, to], redx.at[0, chip % 4], r_ss.at[0], r_rs.at[0], along_row(to))
+                other = (1 - ylo) * 4 + to % 4
+                send(rsend.at[0, other], redx.at[1, chip % 4], r_ss.at[0], r_rs.at[0], along_row(to))
+        else:
+            red[chip] = rsend[jb, chip]
+            for to in chips:
+                send(rsend.at[jb, to], red.at[chip], r_ss.at[jb], r_rs.at[jb], along_row(to))
+
+    def db_cross():
+        wait_for(rsend.at[0, pl.ds(0, 6)], r_rs.at[0])
+        total = redx[1, 0].astype(F32)
+        for o in range(1, 4):
+            total = total + redx[1, o].astype(F32)
+        ysend[...] = total
+        send(ysend, yrecv, y_ss, y_rs, along_row(y_chip))
 
     def db_to_owner(jb):
-        wait_for(red.at[jb, pl.ds(0, NCHIP - 1)], r_rs.at[jb])
-        total = red[jb, 0].astype(F32)
-        for o in range(1, NCHIP):
-            total = total + red[jb, o].astype(F32)
+        if jb == 0:
+            wait_for(yrecv, y_rs)
+            total = yrecv[...]
+            for o in range(4):
+                total = total + redx[0, o].astype(F32)
+        else:
+            wait_for(red.at[pl.ds(0, NCHIP - 1)], r_rs.at[jb])
+            total = red[0].astype(F32)
+            for o in range(1, NCHIP):
+                total = total + red[o].astype(F32)
         lane = lax.broadcasted_iota(jnp.int32, (32, 128), 1)
         for e in range(2):
             to = jb * 4 + core * 2 + e
@@ -305,26 +332,23 @@
             wait_for(bias_full.at[pl.ds(0, 4), pl.ds(0, 32)], b3_rs.at[jb])
             mask_bias(jb)
 
-        @pl.when((jb == 0) & (u < NU - 1))
-        def _():
-            forward(u + 1)
+        @pl.when(it < NU - 1)
+        def _():
+            forward(it + 1)
+
+        tile(u, jb)
+
+        @pl.when(u == NU - 1)
+        def _():
+            db_to_sibling(jb)
+
+        @pl.when(it == NP - 1)
+        def _():
+            db_over_row(0)
 
         @pl.when((jb == 1) & (u > 0))
         def _():
             combine(2 * u - 2)
-
-        tile(jb)
-
-        @pl.when(u == NU - 1)
-        def _():
-            db_to_sibling(jb)
-
-        @pl.when(it == NP - 1)
-        def _():
-            db_over_row(0)
-
-        @pl.when((jb == 1) & (u > 0))
-        def _():
             combine(2 * u - 1)
 
         @pl.when(jb == 1)
@@ -333,10 +357,12 @@
             finish_q(u)
 
     db_over_row(1)
+    db_cross()
     combine(NP - 2)
+    combine(NP - 1)
     db_to_owner(0)
-    combine(NP - 1)
     db_to_owner(1)
+    wait_for(ysend, y_ss)
     owner = (z // 2) % 2 == core
 
     @pl.when(owner)
@@ -365,7 +391,7 @@
         wait_for(bias_full.at[pl.ds(0, 4), pl.ds(0, 16), pl.ds(0, 256)], by_ss.at[jb])
         wait_for(bias_full.at[pl.ds(0, 4), pl.ds(0, 32)], b3_ss.at[jb])
         wait_for(sib.at[jb], a_ss.at[jb])
-        wait_for(red.at[jb, pl.ds(0, NCHIP - 1)], r_ss.at[jb])
+        wait_for(rsend.at[jb, pl.ds(0, NCHIP - 1 if jb else 6)], r_ss.at[jb])
 
 
 def unpack(gq, gkv, fin, dq_out, dk_out, dv_out, db_out):
@@ -407,9 +433,10 @@
             jax.ShapeDtypeStruct((NP, NZ, 32, 128), BF16),
             jax.ShapeDtypeStruct((NZ, 32, 128), F32),
         ),
-        in_specs=[pl.BlockSpec(memory_space=pltpu.SMEM)] + [vm] * 5,
+        in_specs=[pl.BlockSpec(memory_space=pltpu.SMEM)] + [pl.BlockSpec(memory_space=pl.ANY)] * 5,
         out_specs=(vm, vm, vm),
-        scratch_shapes=[
+        scratch_shapes=[V(query.shape, BF16)] * 4
+        + [
             V((NU, 2, NZ, BLK, 128), BF16),
             V((NU, SEQ, 128), BF16),
             V((NU, HALF, 128), BF16),
@@ -417,7 +444,6 @@
             V((HALF, SEQ), F32),
             V((128, SEQ), BF16),
             V((128, HALF), BF16),
-            V((4, HALF, 128), BF16),
             V((2, B, SEQ), F32),
             V((2, B, SEQ), F32),
             V((2, B, SEQ), BF16),
@@ -432,7 +458,10 @@
             V((HALF, SEQ), F32),
             V((NJ, SUB, SEQ), F32),
             V((NJ, NCHIP, SUB, 128), BF16),
-            V((NJ, NCHIP, SUB, 128), BF16),
+            V((NCHIP, SUB, 128), BF16),
+            V((2, 4, SUB, 128), BF16),
+            V((SUB, 128), F32),
+            V((SUB, 128), F32),
             V((NZ, 32, 128), F32),
         ]
         + [D((NU,))] * 6
@@ -442,7 +471,8 @@
         + [D((NU,))] * 2
         + [D((NP,))] * 2
         + [D((NJ,))] * 4
-        + [D] * 2,
+        + [D] * 4
+        + [D((4,))],
         compiler_params=pltpu.CompilerParams(
             vmem_limit_bytes=60 * 2**20, collective_id=0, has_side_effects=True
         ),

time: 64.8 us -> 62.7 us (0.968)
  Pallas kernels: 64.1 us -> 61.9 us
    pallas_call x1, Pallas kernels: 61.1 us -> 59 us  [per_device(): pl.pallas_call(kernel, out_shape=(jax.ShapeDtypeStruct((NU, NZ, 32, 128),...]
where the time goes in v5:
time: 62.7 us; the launch traced here: 62.6 us
  Pallas kernels  61.9 us (99%)
  between operations  0.64 us (1%)
    pallas_call x1, Pallas kernels, per_device(): pl.pallas_call(kernel, out_shape=(jax.ShapeDtypeStruct((NU, NZ, 32, 128),...  59 us
    pallas_call x1, Pallas kernels, per_device(): pl.pallas_call(unpack, grid=(2,), out_shape=(grad, grad, grad, jax.ShapeD...  2.95 us

profile of v5, /device:TPU:1, one launch (start us, length us, event | category | flops | bytes accessed | tf_op | source)
XLA Modules:
  0.0 62.6 jit_solution(16276100117035666723)
XLA Ops:
  0.6 59.0 %shard_map.93 = (bf16[3,8,32,128]{3,2,1,0:T(8,128)(2,1)}, bf16[6,8,32,128]{3,2,1,0:T(8,128)(2,1)}, f32[8,32,128]{2,1,0:T(8,128)}) custom-call(s32[2]{0:T(128)} %len_ref.1, bf16[2,6,64,128]{3,2,1,0:T(8,128)(2,1)} %q_hbm.1, bf16[2,6,64,128]{3,2,1,0:T(8,128)(2,1)} %k_hbm.1, bf16[2,6,64,128]{3,2,1,0:T(8,128)(2,1)} %v_hbm.1, bf16[2,6,64,128]{3,2,1,0:T(8,128)(2,1)} %g_hbm.1, ...), custom_call_target="tpu_custom_call" | custom-call | flops 8000000000 | bytes 4000000 | tf_op jit(solution)/shard_map/pallas_call | solution.py:429
  59.6 2.9 %shard_map.94 = (f32[2,6,64,128]{3,2,1,0:T(8,128)}, f32[2,6,64,128]{3,2,1,0:T(8,128)}, f32[2,6,64,128]{3,2,1,0:T(8,128)}, f32[2,4,64,64]{3,2,1,0:T(8,128)}) custom-call(bf16[3,8,32,128]{3,2,1,0:T(8,128)(2,1)} %get-tuple-element.7.gq, bf16[6,8,32,128]{3,2,1,0:T(8,128)(2,1)} %get-tuple-element.8.gkv, f32[8,32,128]{2,1,0:T(8,128)} %get-tuple-element.9.fin), custom_call_target="tpu_custom_call" | custom-call | tf_op jit(solution)/shard_map/pallas_call | solution.py:483

commit v6 on v5

--- a/solution.py
+++ b/solution.py
@@ -126,8 +126,9 @@
 
     def bias_to_chips(jb):
         mine = bias_full.at[pl.ds(jb * 4, 4), my_rows, my_lanes]
-        send(mine, mine, by_ss.at[jb], by_rs.at[jb], along_row(y_chip))
-        for to in x_chips:
+        if jb == 1:
+            send(mine, mine, by_ss.at[jb], by_rs.at[jb], along_row(y_chip))
+        for to in x_chips if jb == 1 else chips:
             send(mine, mine, b2_ss.at[jb], b2_rs.at[jb], along_row(to))
 
     def bias_onward(jb):
@@ -137,14 +138,13 @@
             send(theirs, theirs, b2_ss.at[jb], b2_rs.at[jb], along_row(to))
 
     def bias_to_sibling(jb):
-        wait_for(bias_full.at[pl.ds(0, 6), :, pl.ds(0, 256)], b2_rs.at[jb])
+        wait_for(bias_full.at[pl.ds(0, 6 if jb else 7), :, pl.ds(0, 256)], b2_rs.at[jb])
         mine = bias_full.at[pl.ds(jb * 4, 4), at(core, 32)]
         send(mine, mine, b3_ss.at[jb], b3_rs.at[jb], sibling)
 
     for load in loads:
         load.wait()
     pack(0)
-    pack(1)
     pl.semaphore_wait(barrier, len(everyone))
     for to in others:
         send(
@@ -160,6 +160,7 @@
     own.start()
     send_kv(0)
     send_qd(0)
+    pack(1)
     own.wait()
     wait_for(bias_full.at[pl.ds(0, NZ - 1), pl.ds(0, 16), pl.ds(0, 256)], b1_rs)
     bias_to_chips(0)
@@ -169,7 +170,6 @@
     send_kv(2)
     send_qd(1)
     send_qd(2)
-    bias_onward(0)
     bias_onward(1)
     forward(0)
     bias_to_sibling(0)
@@ -387,8 +387,9 @@
         wait_for(gkv.at[p, pl.ds(0, NZ - 1)], gk_ss.at[p])
         wait_for(psend.at[p], p_ss.at[p])
     for jb in range(NJ):
-        wait_for(bias_full.at[pl.ds(0, 6), :, pl.ds(0, 256)], b2_ss.at[jb])
-        wait_for(bias_full.at[pl.ds(0, 4), pl.ds(0, 16), pl.ds(0, 256)], by_ss.at[jb])
+        wait_for(bias_full.at[pl.ds(0, 6 if jb else 7), :, pl.ds(0, 256)], b2_ss.at[jb])
+        if jb == 1:
+            wait_for(bias_full.at[pl.ds(0, 4), pl.ds(0, 16), pl.ds(0, 256)], by_ss.at[jb])
         wait_for(bias_full.at[pl.ds(0, 4), pl.ds(0, 32)], b3_ss.at[jb])
         wait_for(sib.at[jb], a_ss.at[jb])
         wait_for(rsend.at[jb, pl.ds(0, NCHIP - 1 if jb else 6)], r_ss.at[jb])

time: 62.7 us -> 61.9 us (0.987)
  Pallas kernels: 61.9 us -> 61 us
    pallas_call x1, Pallas kernels: 59 us -> 58.1 us  [per_device(): pl.pallas_call(kernel, out_shape=(jax.ShapeDtypeStruct((NU, NZ, 32, 128),...]
where the time goes in v6:
time: 61.9 us; the launch traced here: 61.7 us
  Pallas kernels  61 us (99%)
  between operations  0.64 us (1%)
    pallas_call x1, Pallas kernels, per_device(): pl.pallas_call(kernel, out_shape=(jax.ShapeDtypeStruct((NU, NZ, 32, 128),...  58.1 us
    pallas_call x1, Pallas kernels, per_device(): pl.pallas_call(unpack, grid=(2,), out_shape=(grad, grad, grad, jax.ShapeD...  2.95 us

profile of v6, /device:TPU:1, one launch (start us, length us, event | category | flops | bytes accessed | tf_op | source)
XLA Modules:
  0.0 61.7 jit_solution(11297499073638103798)
XLA Ops:
  0.6 58.1 %shard_map.93 = (bf16[3,8,32,128]{3,2,1,0:T(8,128)(2,1)}, bf16[6,8,32,128]{3,2,1,0:T(8,128)(2,1)}, f32[8,32,128]{2,1,0:T(8,128)}) custom-call(s32[2]{0:T(128)} %len_ref.1, bf16[2,6,64,128]{3,2,1,0:T(8,128)(2,1)} %q_hbm.1, bf16[2,6,64,128]{3,2,1,0:T(8,128)(2,1)} %k_hbm.1, bf16[2,6,64,128]{3,2,1,0:T(8,128)(2,1)} %v_hbm.1, bf16[2,6,64,128]{3,2,1,0:T(8,128)(2,1)} %g_hbm.1, ...), custom_call_target="tpu_custom_call" | custom-call | flops 8000000000 | bytes 4000000 | tf_op jit(solution)/shard_map/pallas_call | solution.py:430
  58.7 2.9 %shard_map.94 = (f32[2,6,64,128]{3,2,1,0:T(8,128)}, f32[2,6,64,128]{3,2,1,0:T(8,128)}, f32[2,6,64,128]{3,2,1,0:T(8,128)}, f32[2,4,64,64]{3,2,1,0:T(8,128)}) custom-call(bf16[3,8,32,128]{3,2,1,0:T(8,128)(2,1)} %get-tuple-element.7.gq, bf16[6,8,32,128]{3,2,1,0:T(8,128)(2,1)} %get-tuple-element.8.gkv, f32[8,32,128]{2,1,0:T(8,128)} %get-tuple-element.9.fin), custom_call_target="tpu_custom_call" | custom-call | tf_op jit(solution)/shard_map/pallas_call | solution.py:484

commit v7 on v6

--- a/solution.py
+++ b/solution.py
@@ -170,8 +170,8 @@
     send_kv(2)
     send_qd(1)
     send_qd(2)
+    forward(0)
     bias_onward(1)
-    forward(0)
     bias_to_sibling(0)
     n = len_ref[z // H]
     db[...] = jnp.zeros_like(db)

time: 61.9 us -> 60.7 us (0.981)
  Pallas kernels: 61 us -> 59.8 us
    pallas_call x1, Pallas kernels: 58.1 us -> 56.9 us  [per_device(): pl.pallas_call(kernel, out_shape=(jax.ShapeDtypeStruct((NU, NZ, 32, 128),...]
where the time goes in v7:
time: 60.7 us; the launch traced here: 60.5 us
  Pallas kernels  59.8 us (99%)
  between operations  0.64 us (1%)
    pallas_call x1, Pallas kernels, per_device(): pl.pallas_call(kernel, out_shape=(jax.ShapeDtypeStruct((NU, NZ, 32, 128),...  56.9 us
    pallas_call x1, Pallas kernels, per_device(): pl.pallas_call(unpack, grid=(2,), out_shape=(grad, grad, grad, jax.ShapeD...  2.95 us

profile of v7, /device:TPU:1, one launch (start us, length us, event | category | flops | bytes accessed | tf_op | source)
XLA Modules:
  0.0 60.5 jit_solution(15337461470956656666)
XLA Ops:
  0.6 56.9 %shard_map.93 = (bf16[3,8,32,128]{3,2,1,0:T(8,128)(2,1)}, bf16[6,8,32,128]{3,2,1,0:T(8,128)(2,1)}, f32[8,32,128]{2,1,0:T(8,128)}) custom-call(s32[2]{0:T(128)} %len_ref.1, bf16[2,6,64,128]{3,2,1,0:T(8,128)(2,1)} %q_hbm.1, bf16[2,6,64,128]{3,2,1,0:T(8,128)(2,1)} %k_hbm.1, bf16[2,6,64,128]{3,2,1,0:T(8,128)(2,1)} %v_hbm.1, bf16[2,6,64,128]{3,2,1,0:T(8,128)(2,1)} %g_hbm.1, ...), custom_call_target="tpu_custom_call" | custom-call | flops 8000000000 | bytes 4000000 | tf_op jit(solution)/shard_map/pallas_call | solution.py:430
  57.5 2.9 %shard_map.94 = (f32[2,6,64,128]{3,2,1,0:T(8,128)}, f32[2,6,64,128]{3,2,1,0:T(8,128)}, f32[2,6,64,128]{3,2,1,0:T(8,128)}, f32[2,4,64,64]{3,2,1,0:T(8,128)}) custom-call(bf16[3,8,32,128]{3,2,1,0:T(8,128)(2,1)} %get-tuple-element.7.gq, bf16[6,8,32,128]{3,2,1,0:T(8,128)(2,1)} %get-tuple-element.8.gkv, f32[8,32,128]{2,1,0:T(8,128)} %get-tuple-element.9.fin), custom_call_target="tpu_custom_call" | custom-call | tf_op jit(solution)/shard_map/pallas_call | solution.py:484

commit v8 on v7

--- a/solution.py
+++ b/solution.py
@@ -323,6 +323,10 @@
         def _():
             prep(u)
 
+        @pl.when(it < NU - 1)
+        def _():
+            forward(it + 1)
+
         @pl.when(u == 0)
         def _():
             @pl.when(jb == 0)
@@ -331,10 +335,6 @@
 
             wait_for(bias_full.at[pl.ds(0, 4), pl.ds(0, 32)], b3_rs.at[jb])
             mask_bias(jb)
-
-        @pl.when(it < NU - 1)
-        def _():
-            forward(it + 1)
 
         tile(u, jb)
 

time: 60.7 us -> 60.7 us (level)
  no operation moved by 1% of the time
where the time goes in v8:
time: 60.7 us; the launch traced here: 60.6 us
  Pallas kernels  59.9 us (99%)
  between operations  0.64 us (1%)
    pallas_call x1, Pallas kernels, per_device(): pl.pallas_call(kernel, out_shape=(jax.ShapeDtypeStruct((NU, NZ, 32, 128),...  57 us
    pallas_call x1, Pallas kernels, per_device(): pl.pallas_call(unpack, grid=(2,), out_shape=(grad, grad, grad, jax.ShapeD...  2.95 us

profile of v8, /device:TPU:1, one launch (start us, length us, event | category | flops | bytes accessed | tf_op | source)
XLA Modules:
  0.0 60.6 jit_solution(8608871660598925986)
XLA Ops:
  0.6 57.0 %shard_map.93 = (bf16[3,8,32,128]{3,2,1,0:T(8,128)(2,1)}, bf16[6,8,32,128]{3,2,1,0:T(8,128)(2,1)}, f32[8,32,128]{2,1,0:T(8,128)}) custom-call(s32[2]{0:T(128)} %len_ref.1, bf16[2,6,64,128]{3,2,1,0:T(8,128)(2,1)} %q_hbm.1, bf16[2,6,64,128]{3,2,1,0:T(8,128)(2,1)} %k_hbm.1, bf16[2,6,64,128]{3,2,1,0:T(8,128)(2,1)} %v_hbm.1, bf16[2,6,64,128]{3,2,1,0:T(8,128)(2,1)} %g_hbm.1, ...), custom_call_target="tpu_custom_call" | custom-call | flops 8000000000 | bytes 4000000 | tf_op jit(solution)/shard_map/pallas_call | solution.py:430
  57.6 2.9 %shard_map.94 = (f32[2,6,64,128]{3,2,1,0:T(8,128)}, f32[2,6,64,128]{3,2,1,0:T(8,128)}, f32[2,6,64,128]{3,2,1,0:T(8,128)}, f32[2,4,64,64]{3,2,1,0:T(8,128)}) custom-call(bf16[3,8,32,128]{3,2,1,0:T(8,128)(2,1)} %get-tuple-element.7.gq, bf16[6,8,32,128]{3,2,1,0:T(8,128)(2,1)} %get-tuple-element.8.gkv, f32[8,32,128]{2,1,0:T(8,128)} %get-tuple-element.9.fin), custom_call_target="tpu_custom_call" | custom-call | tf_op jit(solution)/shard_map/pallas_call | solution.py:484
